TPU v7x, 32 devices: a whole 2x2x4 slice. The times are simulated.
32 devices in a mesh: member: 2 (over y), lon: 8 (over z, x), lat: 2 (over core).
Axes of the slice: x: 2, y: 2, z: 4, core: 2. Of those that a mesh axis runs over, the one named last changes fastest.
Arguments:
- saved: float32 [128, 32, 640], P(('member', 'lat'), 'lon'), parts along dimension 0, may hold values from -6 to 6
- cotangent: float32 [128, 32, 640], P(('member', 'lat'), 'lon'), parts along dimension 0, may hold values from -6 to 6
- weight: float32 [640, 640], replicated, may hold values from -0.25 to 0.25
- coefs: float32 [27, 64, 640], P(None, None, 'lon'), may hold values from -1.25 to 1.25
- lon_step: int32 [64], replicated, may hold values from 1 to 8
- row_reach: int32 [64], replicated, may hold values from 1 to 4
Outputs:
- grad_input: float32 [640, 128, 32], P('lon', ('member', 'lat')), parts along dimension 1
- grad_weight: float32 [1280, 640], P(('member', 'lon'), 'lat'), parts along dimension 0
There are 2 independent parts, one for each index of `member`. A program takes and returns all parts, laid end to end along the dimension named above; an argument that names none is the same for every part. Nothing has to cross between parts.
All inputs are finite; a program needn't handle non-finite values.
Results may differ from a plain program's by a relative error of at most 0.00007.
Values sent between devices are 32-bit elements; how exact they have to be, the bound alone decides.
A program may use at most 64 MiB of HBM per device.

v0:
```python
import math

import jax
import jax.numpy as jnp
from jax import lax
from jax.sharding import PartitionSpec as P


def with_halo(x, sides, width):
    for axis, dim in sides:
        peers, length = (lax.axis_size(axis), x.shape[dim])
        up = [(i, (i + 1) % peers) for i in range(peers - 1)]
        down = [(j, i) for i, j in up]
        last = lax.slice_in_dim(x, length - width, length, axis=dim)
        initial = lax.slice_in_dim(x, 0, width, axis=dim)
        before = lax.ppermute(last, axis, up)
        after = lax.ppermute(initial, axis, down)
        x = jnp.concatenate([before, x, after], axis=dim)
    return x


def gelu_slope(values):
    cumulative = 0.5 * (1.0 + lax.erf(values * (1.0 / math.sqrt(2.0))))
    density = jnp.exp(-0.5 * values * values) * (1.0 / math.sqrt(2.0 * math.pi))
    return cumulative + values * density


def shift_rows(gradient, shifts, direction):
    width = gradient.shape[2]
    if direction == 0:
        return gradient
    wrapped = jnp.concatenate([gradient[:, :, width - 8 :], gradient, gradient[:, :, :8]], axis=2)
    result = gradient
    for amount in range(1, 9):
        begin = 8 - direction * amount
        piece = wrapped[:, :, begin : begin + width]
        result = jnp.where((shifts == amount)[None, :, None], piece, result)
    return result


def tap_term(rolled, coefs, row_reach, offset):
    summed = jnp.zeros_like(rolled[0])
    for lon_side in range(3):
        tap_index = (offset + 4) * 3 + lon_side
        summed = summed + jnp.transpose(coefs[tap_index])[:, :, None] * rolled[lon_side]
    live_rows = (abs(offset) <= row_reach).astype(jnp.float32)
    return summed * live_rows[None, :, None]


def body(saved, cotangent, weight, coefs, lon_step, row_reach):
    lat_rows, lon_cols, channels = saved.shape
    lon_devices = lax.axis_size("lon")
    lat_devices = lax.axis_size("lat")
    own_channels = channels // lon_devices
    all_lon = lon_devices * lon_cols
    flat_rows = saved.reshape(lat_rows * lon_cols, channels)
    hidden = jnp.dot(
        flat_rows, weight, precision=lax.Precision.HIGHEST, preferred_element_type=jnp.float32
    )
    pre_grad = cotangent.reshape(lat_rows * lon_cols, channels) * gelu_slope(hidden)
    scale_factor = 1.0 / math.sqrt(lat_rows * lat_devices * all_lon)
    cell_grad = lax.dot_general(
        weight,
        pre_grad,
        (((1,), (1,)), ((), ())),
        precision=lax.Precision.HIGHEST,
        preferred_element_type=jnp.float32,
    )
    moved = lax.all_to_all(cell_grad, "lon", split_axis=0, concat_axis=1, tiled=True)
    gradient = (
        moved.reshape(own_channels, lon_devices, lat_rows, lon_cols)
        .transpose(0, 2, 1, 3)
        .reshape(own_channels, lat_rows, all_lon)
    )
    own_block = lax.psum_scatter(
        lax.dot_general(
            flat_rows,
            pre_grad,
            (((0,), (0,)), ((), ())),
            precision=lax.Precision.HIGHEST,
            preferred_element_type=jnp.float32,
        ),
        "lon",
        scatter_dimension=0,
        tiled=True,
    )
    grad_weight = lax.psum_scatter(own_block, "lat", scatter_dimension=1, tiled=True) * scale_factor
    row_start = lax.axis_index("lat") * lat_rows
    extended = with_halo(gradient, (("lat", 1),), 4)
    steps_padded = jnp.pad(lon_step, 4, constant_values=1)
    reach_padded = jnp.pad(row_reach, 4)
    coefs_padded = jnp.pad(coefs, ((0, 0), (4, 4), (0, 0)))
    wide_steps = lax.dynamic_slice_in_dim(steps_padded, row_start, lat_rows + 8)
    wide_reach = lax.dynamic_slice_in_dim(reach_padded, row_start, lat_rows + 8)
    wide_coefs = lax.dynamic_slice_in_dim(coefs_padded, row_start, lat_rows + 8, 1)
    rolled = [shift_rows(extended, wide_steps, lon_side) for lon_side in (-1, 0, 1)]
    result = jnp.zeros((own_channels, lat_rows, all_lon), jnp.float32)
    for offset in range(-4, 5):
        tap_sum = tap_term(rolled, wide_coefs, wide_reach, offset)
        result = result + tap_sum[:, 4 - offset : 4 - offset + lat_rows]
    return (result, grad_weight)


def solution(mesh):
    placed = (
        P(("member", "lat"), "lon", None),
        P(("member", "lat"), "lon", None),
        P(),
        P(None, None, "lon"),
        P(),
        P(),
    )
    return jax.shard_map(
        body,
        mesh=mesh,
        in_specs=placed,
        out_specs=(P("lon", ("member", "lat"), None), P(("member", "lon"), "lat")),
        check_vma=False,
    )
```

profile of v0, /device:TPU:0, one launch (start us, length us, event | category | flops | bytes accessed | tf_op | source)
XLA Modules:
  0.0 105.5 jit_solution(1087797070094945140)
XLA Ops:
  7.2 1.2 %reshape.61 = f32[128,640]{1,0:T(8,128)S(1)} reshape(f32[32,4,640]{2,1,0:T(4,128)} %param.6) | data formatting | bytes 655360 | tf_op jit(solution)/shard_map/reshape | solution.py:56
  8.4 1.9 %reshape.60 = f32[128,640]{1,0:T(8,128)} reshape(f32[32,4,640]{2,1,0:T(4,128)} %param.7) | data formatting | bytes 655360 | tf_op jit(solution)/shard_map/reshape | solution.py:60
  10.4 1.2 %fusion.99 = f32[128,640]{1,0:T(8,128)S(1)} fusion(f32[128,640]{1,0:T(8,128)S(1)} %reshape.61, f32[640,640]{1,0:T(8,128)S(1)} %copy-done), kind=kOutput, calls=%fused_computation.175 | convolution fusion | flops 629145600 | bytes 2293760 | tf_op jit(solution)/shard_map/dot_general | solution.py:57
  11.6 0.7 copy-done.2
  12.3 2.5 %convolution_bitcast_fusion = f32[640,640]{0,1:T(8,128)S(1)} fusion(f32[128,640]{1,0:T(8,128)} %copy-done.6, f32[128,640]{1,0:T(8,128)S(1)} %copy-done.4, f32[128,640]{1,0:T(8,128)S(1)} %fusion.99), kind=kOutput, calls=%fused_computation | convolution fusion | flops 629882880 | bytes 2621440 | tf_op jit(solution)/shard_map/dot_general | solution.py:76
  14.8 1.7 %copy.26 = f32[640,640]{1,0:T(8,128)} copy(f32[640,640]{0,1:T(8,128)S(1)} %convolution_bitcast_fusion) | data formatting | bytes 3276800
  16.6 0.9 copy-done.3
  17.6 1.7 %convolution_bitcast_fusion.1 = f32[640,128]{0,1:T(8,128)S(1)} fusion(f32[640,640]{1,0:T(8,128)S(1)} %copy-done, f32[128,640]{1,0:T(8,128)S(1)} %copy-done.5, f32[128,640]{1,0:T(8,128)S(1)} %copy-done.3), kind=kOutput, calls=%fused_computation.1 | convolution fusion | flops 629882880 | bytes 2621440 | tf_op jit(solution)/shard_map/dot_general | solution.py:62
  19.3 0.9 copy.21
  20.2 7.2 %all-to-all-start = ((f32[8,80,128]{2,1,0:T(8,128)}), f32[8,80,128]{2,1,0:T(8,128)S(1)}, u32[]{:S(2)}, u32[]{:S(2)}) async-start(f32[8,80,128]{2,1,0:T(8,128)} %bitcast.3), calls=%async_computation | async-start | bytes 655360 | tf_op jit(solution)/shard_map/all_to_all | solution.py:69
  27.5 0.7 compare_convert_fusion
  28.2 0.6 fusion.56
  28.9 0.7 fusion.95
  29.6 0.7 fusion.58
  30.3 0.7 fusion.97
  31.0 0.6 broadcast_compare_fusion.6
  31.6 12.8 %all-to-all-done = f32[8,80,128]{2,1,0:T(8,128)S(1)} async-done(((f32[8,80,128]{2,1,0:T(8,128)}), f32[8,80,128]{2,1,0:T(8,128)S(1)}, u32[]{:S(2)}, u32[]{:S(2)}) %all-to-all-start) | async-done | bytes 327712 | tf_op jit(solution)/shard_map/all_to_all | solution.py:69
  44.4 0.2 copy.22
  44.7 0.3 copy.23
  45.1 1.3 %collective-permute-start = (f32[80,4,32]{0,1,2:T(4,128)S(1)}, f32[80,4,32]{0,1,2:T(4,128)S(1)}, u32[]{:S(2)}, u32[]{:S(2)}) collective-permute-start(f32[80,4,32]{0,1,2:T(4,128)S(1)} %get-tuple-element.47), channel_id=1, source_target_pairs={{0,1},{2,3},{4,5},{6,7},{8,9},{10,11},{12,13},{14,15},{16,17},{18,... | collective-permute-start | bytes 122888 | tf_op jit(solution)/shard_map/ppermute | solution.py:16
  46.4 1.3 %collective-permute-start.1 = (f32[80,4,32]{0,1,2:T(4,128)S(1)}, f32[80,4,32]{0,1,2:T(4,128)S(1)}, u32[]{:S(2)}, u32[]{:S(2)}) collective-permute-start(f32[80,4,32]{0,1,2:T(4,128)S(1)} %get-tuple-element.48), channel_id=1, source_target_pairs={{1,0},{3,2},{5,4},{7,6},{9,8},{11,10},{13,12},{15,14},{17,16},{19,... | collective-permute-start | bytes 122888 | tf_op jit(solution)/shard_map/ppermute | solution.py:17
  48.2 1.3 %collective-permute-done.1 = f32[80,4,32]{0,1,2:T(4,128)S(1)} collective-permute-done((f32[80,4,32]{0,1,2:T(4,128)S(1)}, f32[80,4,32]{0,1,2:T(4,128)S(1)}, u32[]{:S(2)}, u32[]{:S(2)}) %collective-permute-start.1) | collective-permute-done | bytes 40992 | tf_op jit(solution)/shard_map/ppermute | solution.py:17
  49.8 0.5 copy-done.17
  50.3 0.3 fusion.13
  50.7 1.2 %fusion.6 = f32[80,40,32]{0,1,2:T(8,128)} fusion(f32[80,40,40]{0,1,2:T(8,128)S(1)} %get-tuple-element.44, pred[40]{0:T(512)(128)(4,1)S(1)} %copy-done.20, pred[40]{0:T(512)(128)(4,1)S(1)} %get-tuple-element.62, pred[40]{0:T(512)(128)(4,1)S(1)} %get-tuple-element.63, pred[40]{0:T(512)(128)(4,1)S(1)} %copy-done.17, pred[40]{0:T(512)(128)(4,1)S(1)} %copy-done.18, ...), kind=kLoop, calls=%fused_computation.38 | loop fusion | flops 1024000 | bytes 4096320 | tf_op jit(solution)/shard_map/jit(_where)/select_n | solution.py:37
  51.9 36.0 %reduce-scatter.7.cloned.1.call-done = f32[80,640]{1,0:T(8,128)} async-done(((f32[640,640]{1,0:T(8,128)}), f32[80,640]{1,0:T(8,128)}) %reduce-scatter.7.cloned.1.call-update) | async-done | bytes 204816
  87.9 1.8 %copy.27 = f32[80,640]{0,1:T(8,128)} copy(f32[80,640]{1,0:T(8,128)} %reduce-scatter.7.cloned.1.call-done) | data formatting | bytes 409600
  89.8 5.3 %fusion.16 = f32[80,32,32]{0,1,2:T(8,128)S(1)} fusion(f32[80,40,32]{0,1,2:T(8,128)} %fusion.6, f32[80,40,32]{0,1,2:T(8,128)S(1)} %pad_maximum_fusion.1, f32[80,40,32]{0,1,2:T(8,128)S(1)} %fusion.13, f32[32]{0:T(128)S(1)} %copy-done.22, f32[80,32]{0,1:T(8,128)S(1)} %slice.322, f32[80,32]{0,1:T(8,128)S(1)} %slice.320, f32[80,32]{0,1:T(8,128)S(1)} %slice.318, ...), kind=kLoop, calls=%fused_computation.51 | loop fusion | flops 5079040 | bytes 9452672 | tf_op jit(solution)/shard_map/add | solution.py:100
  95.1 1.1 %copy.24 = f32[80,32,32]{0,2,1:T(8,128)} copy(f32[80,32,32]{0,1,2:T(8,128)S(1)} %fusion.16) | data formatting | bytes 655360
  96.2 0.7 reduce-scatter.5.cloned.1.call-done
  96.9 0.9 broadcast_multiply_fusion
  97.9 0.8 copy.25
  (101 shorter events, 1.0 us)
Async XLA Ops:
  7.2 3.2 %copy-start = (f32[640,640]{1,0:T(8,128)S(1)}, f32[640,640]{1,0:T(8,128)}, u32[]{:S(2)}) copy-start(f32[640,640]{1,0:T(8,128)} %param.8) | copy-start | bytes 4915204
  7.2 80.7 %reduce-scatter.7.cloned.1.call-start = ((), (), s32[]{:S(2)}) async-start(), calls=%async_computation.4 | async-start | bytes 1843200
  8.4 1.9 %copy-start.6 = (f32[128,640]{1,0:T(8,128)}, f32[128,640]{1,0:T(8,128)S(1)}, u32[]{:S(2)}) copy-start(f32[128,640]{1,0:T(8,128)S(1)} %reshape.61) | copy-start | bytes 983044
  10.4 2.0 %copy-start.4 = (f32[128,640]{1,0:T(8,128)S(1)}, f32[128,640]{1,0:T(8,128)}, u32[]{:S(2)}) copy-start(f32[128,640]{1,0:T(8,128)} %reshape.60) | copy-start | bytes 983044
  16.5 1.0 copy-start.3
  16.5 1.1 %copy-start.5 = (f32[128,640]{1,0:T(8,128)S(1)}, f32[128,640]{1,0:T(8,128)}, u32[]{:S(2)}) copy-start(f32[128,640]{1,0:T(8,128)} %reshape.60) | copy-start | bytes 983044
  17.6 9.9 %copy-start.29 = (s32[64]{0:T(128)S(1)}, s32[64]{0:T(128)}, u32[]{:S(2)}) copy-start(s32[64]{0:T(128)} %param.11) | copy-start | bytes 772
  17.6 10.6 %copy-start.1 = (f32[27,64,80]{2,1,0:T(8,128)S(1)}, f32[27,64,80]{2,1,0:T(8,128)}, u32[]{:S(2)}) copy-start(f32[27,64,80]{2,1,0:T(8,128)} %param.9) | copy-start | bytes 1658884
  19.3 10.2 %copy-start.30 = (s32[64]{0:T(128)S(1)}, s32[64]{0:T(128)}, u32[]{:S(2)}) copy-start(s32[64]{0:T(128)} %param.10) | copy-start | bytes 772
  20.2 24.1 %all-to-all-start = ((f32[8,80,128]{2,1,0:T(8,128)}), f32[8,80,128]{2,1,0:T(8,128)S(1)}, u32[]{:S(2)}, u32[]{:S(2)}) async-start(f32[8,80,128]{2,1,0:T(8,128)} %bitcast.3), calls=%async_computation | async-start | bytes 655360 | tf_op jit(solution)/shard_map/all_to_all | solution.py:69
  27.5 69.5 %reduce-scatter.5.cloned.1.call-start = ((), (), s32[]{:S(2)}) async-start(), calls=%async_computation.3 | async-start | bytes 491520 | tf_op jit(solution)/shard_map/reduce_scatter | solution.py:87
  44.6 3.1 %copy-start.16 = (f32[80,40]{0,1:T(8,128)S(1)}, f32[80,40]{0,1:T(8,128)}, u32[]{:S(2)}) copy-start(f32[80,40]{0,1:T(8,128)} %get-tuple-element.25) | copy-start | bytes 38404
  44.6 3.2 %copy-start.15 = (f32[80,40]{0,1:T(8,128)S(1)}, f32[80,40]{0,1:T(8,128)}, u32[]{:S(2)}) copy-start(f32[80,40]{0,1:T(8,128)} %get-tuple-element.33) | copy-start | bytes 38404
  44.6 3.2 %copy-start.14 = (f32[80,40]{0,1:T(8,128)S(1)}, f32[80,40]{0,1:T(8,128)}, u32[]{:S(2)}) copy-start(f32[80,40]{0,1:T(8,128)} %get-tuple-element.32) | copy-start | bytes 38404
  44.6 3.3 %copy-start.13 = (f32[80,40]{0,1:T(8,128)S(1)}, f32[80,40]{0,1:T(8,128)}, u32[]{:S(2)}) copy-start(f32[80,40]{0,1:T(8,128)} %get-tuple-element.31) | copy-start | bytes 38404
  44.6 3.3 %copy-start.12 = (f32[80,40]{0,1:T(8,128)S(1)}, f32[80,40]{0,1:T(8,128)}, u32[]{:S(2)}) copy-start(f32[80,40]{0,1:T(8,128)} %get-tuple-element.30) | copy-start | bytes 38404
  44.6 3.3 %copy-start.11 = (f32[80,40]{0,1:T(8,128)S(1)}, f32[80,40]{0,1:T(8,128)}, u32[]{:S(2)}) copy-start(f32[80,40]{0,1:T(8,128)} %get-tuple-element.29) | copy-start | bytes 38404
  44.7 3.3 %copy-start.10 = (f32[80,40]{0,1:T(8,128)S(1)}, f32[80,40]{0,1:T(8,128)}, u32[]{:S(2)}) copy-start(f32[80,40]{0,1:T(8,128)} %get-tuple-element.28) | copy-start | bytes 38404
  44.7 3.3 %copy-start.9 = (f32[80,40]{0,1:T(8,128)S(1)}, f32[80,40]{0,1:T(8,128)}, u32[]{:S(2)}) copy-start(f32[80,40]{0,1:T(8,128)} %get-tuple-element.27) | copy-start | bytes 38404
  44.7 3.3 %copy-start.8 = (f32[80,40]{0,1:T(8,128)S(1)}, f32[80,40]{0,1:T(8,128)}, u32[]{:S(2)}) copy-start(f32[80,40]{0,1:T(8,128)} %get-tuple-element.26) | copy-start | bytes 38404
  44.7 3.3 %copy-start.7 = (f32[80,40]{0,1:T(8,128)S(1)}, f32[80,40]{0,1:T(8,128)}, u32[]{:S(2)}) copy-start(f32[80,40]{0,1:T(8,128)} %get-tuple-element.16) | copy-start | bytes 38404
  44.7 3.5 %copy-start.31 = (f32[40]{0:T(128)S(1)}, f32[40]{0:T(128)}, u32[]{:S(2)}) copy-start(f32[40]{0:T(128)} %get-tuple-element.12) | copy-start | bytes 484
  45.1 3.2 %collective-permute-start = (f32[80,4,32]{0,1,2:T(4,128)S(1)}, f32[80,4,32]{0,1,2:T(4,128)S(1)}, u32[]{:S(2)}, u32[]{:S(2)}) collective-permute-start(f32[80,4,32]{0,1,2:T(4,128)S(1)} %get-tuple-element.47), channel_id=1, source_target_pairs={{0,1},{2,3},{4,5},{6,7},{8,9},{10,11},{12,13},{14,15},{16,17},{18,... | collective-permute-start | bytes 122888 | tf_op jit(solution)/shard_map/ppermute | solution.py:16
  46.4 3.1 %collective-permute-start.1 = (f32[80,4,32]{0,1,2:T(4,128)S(1)}, f32[80,4,32]{0,1,2:T(4,128)S(1)}, u32[]{:S(2)}, u32[]{:S(2)}) collective-permute-start(f32[80,4,32]{0,1,2:T(4,128)S(1)} %get-tuple-element.48), channel_id=1, source_target_pairs={{1,0},{3,2},{5,4},{7,6},{9,8},{11,10},{13,12},{15,14},{17,16},{19,... | collective-permute-start | bytes 122888 | tf_op jit(solution)/shard_map/ppermute | solution.py:17
  50.7 39.1 %copy-start.21 = (f32[32]{0:T(128)S(1)}, f32[32]{0:T(128)}, u32[]{:S(2)}) copy-start(f32[32]{0:T(128)} %get-tuple-element.49) | copy-start | bytes 388
  50.7 39.1 %copy-start.22 = (f32[32]{0:T(128)S(1)}, f32[32]{0:T(128)}, u32[]{:S(2)}) copy-start(f32[32]{0:T(128)} %get-tuple-element.50) | copy-start | bytes 388
  50.7 39.1 %copy-start.23 = (f32[32]{0:T(128)S(1)}, f32[32]{0:T(128)}, u32[]{:S(2)}) copy-start(f32[32]{0:T(128)} %get-tuple-element.68) | copy-start | bytes 388
  50.7 39.1 %copy-start.24 = (f32[32]{0:T(128)S(1)}, f32[32]{0:T(128)}, u32[]{:S(2)}) copy-start(f32[32]{0:T(128)} %get-tuple-element.69) | copy-start | bytes 388
  50.7 39.1 %copy-start.25 = (f32[32]{0:T(128)S(1)}, f32[32]{0:T(128)}, u32[]{:S(2)}) copy-start(f32[32]{0:T(128)} %get-tuple-element.53) | copy-start | bytes 388
  50.7 39.1 %copy-start.26 = (f32[32]{0:T(128)S(1)}, f32[32]{0:T(128)}, u32[]{:S(2)}) copy-start(f32[32]{0:T(128)} %get-tuple-element.54) | copy-start | bytes 388
  50.7 39.1 %copy-start.27 = (f32[32]{0:T(128)S(1)}, f32[32]{0:T(128)}, u32[]{:S(2)}) copy-start(f32[32]{0:T(128)} %get-tuple-element.70) | copy-start | bytes 388
  50.7 39.1 %copy-start.28 = (f32[32]{0:T(128)S(1)}, f32[32]{0:T(128)}, u32[]{:S(2)}) copy-start(f32[32]{0:T(128)} %get-tuple-element.71) | copy-start | bytes 388
  (5 other events, 3.4 us)
Sparse Core Ops, SparseCore 0:
  16.7 71.1 reduce-scatter.6
  90.2 6.6 reduce-scatter.4
where the time goes:
time: 106 us; the launch traced here: 105 us
  waiting for transfers between devices  50.8 us (48%)
  local copies, waits for them, and re-layouts  15.3 us (14%)
  between operations  14.7 us (14%)
  starting transfers between devices  9.91 us (9%)
  other arithmetic  9.31 us (9%)
  matrix products  5.41 us (5%)
    unnamed x3, waiting for transfers between devices  36 us
    all_to_all x1, waiting for transfers between devices, body(): lax.all_to_all(cell_grad, 'lon', split_axis=0, concat_axis=1, tiled=True)  12.8 us
    unnamed x68, local copies, waits for them, and re-layouts  7.78 us
    all_to_all x1, starting transfers between devices, body(): lax.all_to_all(cell_grad, 'lon', split_axis=0, concat_axis=1, tiled=True)  7.25 us
    add x1, other arithmetic, body(): result = result + tap_sum[:, 4 - offset:4 - offset + lat_rows]  5.28 us
    dot_general x1, matrix products, body(): lax.dot_general(flat_rows, pre_grad, (((0,), (0,)), ((), ())), precision=...  2.48 us
  transfers between devices with their start and end apart: 5, of which 4 were waited for; matrix products, arithmetic and copies ran while one was open for 15% of the time, Pallas kernels for 0%

commit v1 on v0

--- a/solution.py
+++ b/solution.py
@@ -1,9 +1,247 @@
+import functools
 import math
 
 import jax
 import jax.numpy as jnp
 from jax import lax
+from jax.experimental import pallas as pl
+from jax.experimental.pallas import tpu as pltpu
 from jax.sharding import PartitionSpec as P
+
+MESH = pl.DeviceIdType.MESH
+REACH = 4
+MOST_STEP = 8
+
+
+def gelu_slope(values):
+    cumulative = 0.5 * (1.0 + lax.erf(values * (1.0 / math.sqrt(2.0))))
+    density = jnp.exp(-0.5 * values * values) * (1.0 / math.sqrt(2.0 * math.pi))
+    return cumulative + values * density
+
+
+def halves(x):
+    high = x.astype(jnp.bfloat16)
+    low = (x - high.astype(jnp.float32)).astype(jnp.bfloat16)
+    return high, low
+
+
+def dot3(a, b, dims):
+    (ah, al), (bh, bl) = a, b
+    dot = lambda p, q: lax.dot_general(p, q, (dims, ((), ())), preferred_element_type=jnp.float32)
+    return dot(ah, bh) + (dot(ah, bl) + dot(al, bh))
+
+
+def flipped(me, j, n):
+    result = 0
+    bit = 1
+    while bit < n:
+        mine = lax.rem(lax.div(me, bit), 2)
+        result = result + bit * ((1 - mine) if j & bit else mine)
+        bit *= 2
+    return result
+
+
+def zeros_below(j):
+    return (j & -j).bit_length() - 1
+
+
+def kernel(
+    n,
+    step_ref, reach_ref, saved_ref, cot_ref, weight_ref, coefs_ref,
+    acc_out, gw_out,
+    s_t, s_t_peer, pg_t, pg_t_peer, cell, arrived, part, landed, grid_ref, halo, acc,
+    lat_send, lat_recv, a2a_send, a2a_recv, gw_send, gw_recv,
+):
+    me = lax.axis_index("lon")
+    lat = lax.axis_index("lat")
+    other = 1 - lat
+    rows, cols, channels = saved_ref.shape
+    cells = rows * cols
+    own = channels // n
+    half = channels // 2
+    all_lon = n * cols
+    bits = n.bit_length() - 1
+
+    barrier = pltpu.get_barrier_semaphore()
+    for s in range(1, n):
+        pl.semaphore_signal(barrier, inc=1, device_id={"lon": lax.rem(me + s, n)}, device_id_type=MESH)
+    pl.semaphore_signal(barrier, inc=1, device_id={"lat": other}, device_id_type=MESH)
+
+    saved = saved_ref[...].reshape(cells, channels)
+    s_t[...] = saved.T.reshape(n, own, cells)
+    pl.semaphore_wait(barrier, n)
+
+    def to_peer(src, dst, slot):
+        return pltpu.make_async_remote_copy(
+            src_ref=src, dst_ref=dst, send_sem=lat_send.at[slot], recv_sem=lat_recv.at[slot],
+            device_id={"lat": other}, device_id_type=MESH,
+        )
+
+    saved_copy = to_peer(s_t, s_t_peer, 0)
+    saved_copy.start()
+
+    weight = halves(weight_ref[...])
+    hidden = dot3(halves(saved), weight, ((1,), (0,)))
+    pre_grad = cot_ref[...].reshape(cells, channels) * gelu_slope(hidden)
+    turned = pre_grad.T
+    pg_t[...] = turned.reshape(2, half, cells)
+    pg_copy = to_peer(pg_t.at[other], pg_t_peer, 1)
+    pg_copy.start()
+
+    cell[...] = dot3(weight, halves(turned), ((1,), (0,))).reshape(n, own, cells)
+
+    def across(s):
+        dest = lax.rem(me + s, n)
+        return pltpu.make_async_remote_copy(
+            src_ref=cell.at[dest], dst_ref=arrived.at[me], send_sem=a2a_send.at[s - 1], recv_sem=a2a_recv.at[s - 1],
+            device_id={"lon": dest}, device_id_type=MESH,
+        )
+
+    moves = [across(s) for s in range(1, n)]
+    for move in moves:
+        move.start()
+
+    def slot_of(stage, j):
+        return n - (n >> stage) + j // (2 << stage)
+
+    def hand_on(j):
+        stage = zeros_below(j)
+        slot = slot_of(stage, j)
+        return pltpu.make_async_remote_copy(
+            src_ref=part.at[j], dst_ref=landed.at[slot], send_sem=gw_send.at[slot], recv_sem=gw_recv.at[slot],
+            device_id={"lon": flipped(me, 1 << stage, n)}, device_id_type=MESH,
+        )
+
+    order = sorted(range(n), key=lambda j: -int(format(j, "b").zfill(bits)[::-1], 2))
+    sends = {j: hand_on(j) for j in range(1, n)}
+    mine = halves(pg_t[lat])
+    saved_copy.wait_recv()
+    pg_copy.wait_recv()
+    theirs = halves(pg_t_peer[...])
+    for j in order:
+        owner = flipped(me, j, n)
+        part[j] = dot3(halves(s_t[owner]), mine, ((1,), (1,))) + dot3(halves(s_t_peer[owner]), theirs, ((1,), (1,)))
+        if j % 2:
+            sends[j].start()
+
+    def gather(j):
+        total = part[j]
+        for stage in range(bits if j == 0 else zeros_below(j)):
+            came = j + (1 << stage)
+            sends[came].wait_recv()
+            total = total + landed[slot_of(stage, j)]
+        return total
+
+    later = [j for j in order if j % 2 == 0 and j]
+    first = [j for j in later if j % 4]
+    rest = [j for j in later if not j % 4]
+    for j in first:
+        part[j] = gather(j)
+        sends[j].start()
+
+    acc[...] = jnp.zeros_like(acc)
+    arrived[me] = cell[me]
+    for move in moves:
+        move.wait_recv()
+    for source in range(n):
+        grid_ref[:, source * cols : (source + 1) * cols, :] = arrived[source].T.reshape(rows, cols, own)
+
+    halo_copy = pltpu.make_async_remote_copy(
+        src_ref=grid_ref.at[pl.ds((rows - REACH) * other, REACH)], dst_ref=halo,
+        send_sem=lat_send.at[2], recv_sem=lat_recv.at[2],
+        device_id={"lat": other}, device_id_type=MESH,
+    )
+    halo_copy.start()
+
+    for j in rest:
+        part[j] = gather(j)
+        sends[j].start()
+
+    def scatter(values, row, local):
+        step = jnp.full(values.shape, step_ref[row], jnp.int32)
+        reach = reach_ref[row]
+        up = values
+        down = values
+        bit = 1
+        while bit <= MOST_STEP:
+            chosen = (step & bit) != 0
+            up = jnp.where(chosen, jnp.roll(up, bit, axis=0), up)
+            down = jnp.where(chosen, jnp.roll(down, -bit, axis=0), down)
+            bit *= 2
+        rolled = (down, values, up)
+        for offset in range(-REACH, REACH + 1):
+            live = jnp.where(abs(offset) <= reach, 1.0, 0.0).astype(jnp.float32)
+            summed = None
+            for side in range(3):
+                term = coefs_ref[3 * (offset + REACH) + side, pl.ds(row, 1), :] * live * rolled[side]
+                summed = term if summed is None else summed + term
+            acc[local + offset + 2 * REACH] += summed
+
+    @pl.loop(0, rows)
+    def _(i):
+        scatter(grid_ref[i], lat * rows + i, i)
+
+    halo_copy.wait_recv()
+
+    @pl.loop(0, REACH)
+    def _(i):
+        local = rows * other - REACH * lat + i
+        scatter(halo[i], lat * rows + local, local)
+
+    acc_out[...] = acc[2 * REACH : 2 * REACH + rows]
+    gw_out[...] = gather(0)
+
+    saved_copy.wait_send()
+    pg_copy.wait_send()
+    halo_copy.wait_send()
+    for move in moves:
+        move.wait_send()
+    for j in range(1, n):
+        sends[j].wait_send()
+
+
+def kernel_body(saved, cotangent, weight, coefs, lon_step, row_reach):
+    rows, cols, channels = saved.shape
+    n = lax.axis_size("lon")
+    own = channels // n
+    half = channels // 2
+    cells = rows * cols
+    f32 = jnp.float32
+    vmem = pl.BlockSpec(memory_space=pltpu.VMEM)
+    smem = pl.BlockSpec(memory_space=pltpu.SMEM)
+    acc, grad = pl.pallas_call(
+        functools.partial(kernel, n),
+        out_shape=(
+            jax.ShapeDtypeStruct((rows, n * cols, own), f32),
+            jax.ShapeDtypeStruct((own, half), f32),
+        ),
+        in_specs=[smem, smem, vmem, vmem, vmem, vmem],
+        out_specs=(vmem, vmem),
+        scratch_shapes=[
+            pltpu.VMEM((n, own, cells), f32),
+            pltpu.VMEM((n, own, cells), f32),
+            pltpu.VMEM((2, half, cells), f32),
+            pltpu.VMEM((half, cells), f32),
+            pltpu.VMEM((n, own, cells), f32),
+            pltpu.VMEM((n, own, cells), f32),
+            pltpu.VMEM((n, own, half), f32),
+            pltpu.VMEM((n - 1, own, half), f32),
+            pltpu.VMEM((rows, n * cols, own), f32),
+            pltpu.VMEM((REACH, n * cols, own), f32),
+            pltpu.VMEM((rows + 4 * REACH, n * cols, own), f32),
+            pltpu.SemaphoreType.DMA((3,)),
+            pltpu.SemaphoreType.DMA((3,)),
+            pltpu.SemaphoreType.DMA((n - 1,)),
+            pltpu.SemaphoreType.DMA((n - 1,)),
+            pltpu.SemaphoreType.DMA((n - 1,)),
+            pltpu.SemaphoreType.DMA((n - 1,)),
+        ],
+        compiler_params=pltpu.CompilerParams(
+            collective_id=0, has_side_effects=True, vmem_limit_bytes=40 * 1024 * 1024
+        ),
+    )(lon_step, row_reach, saved, cotangent, weight, coefs)
+    scale = 1.0 / math.sqrt(rows * 2 * n * cols)
+    return jnp.transpose(acc, (2, 0, 1)), grad * scale
 
 
 def with_halo(x, sides, width):
@@ -19,12 +257,6 @@
     return x
 
 
-def gelu_slope(values):
-    cumulative = 0.5 * (1.0 + lax.erf(values * (1.0 / math.sqrt(2.0))))
-    density = jnp.exp(-0.5 * values * values) * (1.0 / math.sqrt(2.0 * math.pi))
-    return cumulative + values * density
-
-
 def shift_rows(gradient, shifts, direction):
     width = gradient.shape[2]
     if direction == 0:
@@ -47,7 +279,7 @@
     return summed * live_rows[None, :, None]
 
 
-def body(saved, cotangent, weight, coefs, lon_step, row_reach):
+def collective_body(saved, cotangent, weight, coefs, lon_step, row_reach):
     lat_rows, lon_cols, channels = saved.shape
     lon_devices = lax.axis_size("lon")
     lat_devices = lax.axis_size("lat")
@@ -101,6 +333,22 @@
     return (result, grad_weight)
 
 
+def body(saved, cotangent, weight, coefs, lon_step, row_reach):
+    rows, cols, channels = saved.shape
+    n = lax.axis_size("lon")
+    fits = (
+        lax.axis_size("lat") == 2
+        and 4 <= n <= 16
+        and n & (n - 1) == 0
+        and channels % (16 * n) == 0
+        and (rows * cols) % 128 == 0
+        and rows >= REACH
+        and n * cols >= MOST_STEP
+    )
+    run = kernel_body if fits else collective_body
+    return run(saved, cotangent, weight, coefs, lon_step, row_reach)
+
+
 def solution(mesh):
     placed = (
         P(("member", "lat"), "lon", None),

time: 106 us -> 36.7 us (0.35)
  waiting for transfers between devices: 50.8 us -> 0 us
  Pallas kernels: 0 us -> 28.4 us
  between operations: 14.7 us -> 0.65 us
  starting transfers between devices: 9.91 us -> 0 us
  local copies, waits for them, and re-layouts: 15.3 us -> 6.64 us
  other arithmetic: 9.31 us -> 0.66 us
  matrix products: 5.41 us -> 0 us
    unnamed x3 -> x0, waiting for transfers between devices: 36 us -> none
    pallas_call x0 -> x1, Pallas kernels: none -> 28.4 us  [kernel_body(): pl.pallas_call(functools.partial(kernel, n), out_shape=(jax.ShapeDtypeStr...]
    all_to_all x1 -> x0, waiting for transfers between devices: 12.8 us -> none  [body(): lax.all_to_all(cell_grad, 'lon', split_axis=0, concat_axis=1, tiled=True)]
    all_to_all x1 -> x0, starting transfers between devices: 7.25 us -> none  [body(): lax.all_to_all(cell_grad, 'lon', split_axis=0, concat_axis=1, tiled=True)]
    dot_general x3 -> x0, matrix products: 5.41 us -> none  [the longest x1 2.48 us: body(): lax.dot_general(flat_rows, pre_grad, (((0,), (0,)), ((), ())), precision=...]
    add x1 -> x0, other arithmetic: 5.28 us -> none  [body(): result = result + tap_sum[:, 4 - offset:4 - offset + lat_rows]]
    reshape x2 -> x0, local copies, waits for them, and re-layouts: 3.13 us -> none  [the longest x1 1.93 us: body(): cotangent.reshape(lat_rows * lon_cols, channels) * gelu_slope(hidden)]
    ppermute x2 -> x0, starting transfers between devices: 2.59 us -> none  [the longest x1 1.29 us: with_halo(): before = lax.ppermute(last, axis, up)]
  transfers between devices with their start and end apart: 5 -> 0, of which waited for: 4 -> 0; matrix products, arithmetic and copies ran while one was open for 15% -> 0% of each run, Pallas kernels for 0% -> 0%
where the time goes in v1:
time: 36.7 us; the launch traced here: 36.4 us
  Pallas kernels  28.4 us (77%)
  local copies, waits for them, and re-layouts  6.64 us (18%)
  other arithmetic  0.66 us (2%)
  between operations  0.65 us (2%)
    pallas_call x1, Pallas kernels, kernel_body(): pl.pallas_call(functools.partial(kernel, n), out_shape=(jax.ShapeDtypeStr...  28.4 us
    unnamed x13, local copies, waits for them, and re-layouts  6.64 us

profile of v1, /device:TPU:0, one launch (start us, length us, event | category | flops | bytes accessed | tf_op | source)
XLA Modules:
  0.0 36.4 jit_solution(2050566526185304129)
XLA Ops:
  0.6 0.0 copy-start
  0.6 1.4 %copy-done = f32[640,640]{1,0:T(8,128)S(1)} copy-done((f32[640,640]{1,0:T(8,128)S(1)}, f32[640,640]{1,0:T(8,128)}, u32[]{:S(2)}) %copy-start) | copy-done | bytes 1638424
  2.1 0.0 copy-start.1
  2.1 1.2 %copy-done.1 = f32[27,64,80]{2,1,0:T(8,128)S(1)} copy-done((f32[27,64,80]{2,1,0:T(8,128)S(1)}, f32[27,64,80]{2,1,0:T(8,128)}, u32[]{:S(2)}) %copy-start.1) | copy-done | bytes 552984
  3.2 0.0 copy-start.2
  3.2 1.0 %copy-done.2 = f32[32,4,640]{2,1,0:T(4,128)S(1)} copy-done((f32[32,4,640]{2,1,0:T(4,128)S(1)}, f32[32,4,640]{2,1,0:T(4,128)}, u32[]{:S(2)}) %copy-start.2) | copy-done | bytes 327704
  4.2 0.0 copy-start.3
  4.2 1.0 %copy-done.3 = f32[32,4,640]{2,1,0:T(4,128)S(1)} copy-done((f32[32,4,640]{2,1,0:T(4,128)S(1)}, f32[32,4,640]{2,1,0:T(4,128)}, u32[]{:S(2)}) %copy-start.3) | copy-done | bytes 327704
  5.2 0.0 copy-start.4
  5.2 0.7 %copy-done.4 = s32[64]{0:T(128)S(1)} copy-done((s32[64]{0:T(128)S(1)}, s32[64]{0:T(128)}, u32[]{:S(2)}) %copy-start.4) | copy-done | bytes 280
  5.8 0.0 copy-start.5
  5.8 0.7 %copy-done.5 = s32[64]{0:T(128)S(1)} copy-done((s32[64]{0:T(128)S(1)}, s32[64]{0:T(128)}, u32[]{:S(2)}) %copy-start.5) | copy-done | bytes 280
  6.5 28.4 %shard_map.77 = (f32[32,32,80]{2,1,0:T(8,128)S(1)}, f32[80,320]{1,0:T(8,128)S(1)}) custom-call(s32[64]{0:T(128)S(1)} %copy-done.4, s32[64]{0:T(128)S(1)} %copy-done.5, f32[32,4,640]{2,1,0:T(4,128)S(1)} %copy-done.2, f32[32,4,640]{2,1,0:T(4,128)S(1)} %copy-done.3, f32[640,640]{1,0:T(8,128)S(1)} %copy-done, f32[27,64,80]{2,1,0:T(8,128)S(1)} %copy-done.1), custom_call_target="tpu_custom_call" | custom-call | tf_op jit(solution)/shard_map/pallas_call | solution.py:212
  34.9 0.7 %broadcast_multiply_fusion = f32[80,320]{1,0:T(8,128)} fusion(f32[80,320]{1,0:T(8,128)S(1)} %get-tuple-element.5), kind=kLoop, calls=%fused_computation | loop fusion | flops 25600 | bytes 204800 | tf_op jit(solution)/shard_map/mul | solution.py:244
  35.6 0.8 %copy.9 = f32[80,32,32]{0,2,1:T(8,128)} copy(f32[80,32,32]{0,2,1:T(8,128)S(1)} %bitcast.1) | data formatting | bytes 655360
Async XLA Ops:
  0.6 1.4 %copy-start = (f32[640,640]{1,0:T(8,128)S(1)}, f32[640,640]{1,0:T(8,128)}, u32[]{:S(2)}) copy-start(f32[640,640]{1,0:T(8,128)} %weight_ref.1) | copy-start | bytes 4915204
  2.1 1.2 %copy-start.1 = (f32[27,64,80]{2,1,0:T(8,128)S(1)}, f32[27,64,80]{2,1,0:T(8,128)}, u32[]{:S(2)}) copy-start(f32[27,64,80]{2,1,0:T(8,128)} %coefs_ref.1) | copy-start | bytes 1658884
  3.2 1.0 %copy-start.2 = (f32[32,4,640]{2,1,0:T(4,128)S(1)}, f32[32,4,640]{2,1,0:T(4,128)}, u32[]{:S(2)}) copy-start(f32[32,4,640]{2,1,0:T(4,128)} %saved_ref.1) | copy-start | bytes 983044
  4.2 1.0 %copy-start.3 = (f32[32,4,640]{2,1,0:T(4,128)S(1)}, f32[32,4,640]{2,1,0:T(4,128)}, u32[]{:S(2)}) copy-start(f32[32,4,640]{2,1,0:T(4,128)} %cot_ref.1) | copy-start | bytes 983044
  5.2 0.7 %copy-start.4 = (s32[64]{0:T(128)S(1)}, s32[64]{0:T(128)}, u32[]{:S(2)}) copy-start(s32[64]{0:T(128)} %step_ref.1) | copy-start | bytes 772
  5.8 0.7 %copy-start.5 = (s32[64]{0:T(128)S(1)}, s32[64]{0:T(128)}, u32[]{:S(2)}) copy-start(s32[64]{0:T(128)} %reach_ref.1) | copy-start | bytes 772

commit v2 on v1

--- a/solution.py
+++ b/solution.py
@@ -11,6 +11,7 @@
 MESH = pl.DeviceIdType.MESH
 REACH = 4
 MOST_STEP = 8
+LANES = 128
 
 
 def gelu_slope(values):
@@ -47,8 +48,9 @@
 
 def kernel(
     n,
-    step_ref, reach_ref, saved_ref, cot_ref, weight_ref, coefs_ref,
+    step_in, reach_in, saved_in, cot_in, weight_in, coefs_in,
     acc_out, gw_out,
+    step_ref, reach_ref, saved_ref, cot_ref, weight_ref, coefs_ref, load_sem,
     s_t, s_t_peer, pg_t, pg_t_peer, cell, arrived, part, landed, grid_ref, halo, acc,
     lat_send, lat_recv, a2a_send, a2a_recv, gw_send, gw_recv,
 ):
@@ -61,14 +63,28 @@
     half = channels // 2
     all_lon = n * cols
     bits = n.bit_length() - 1
+    full, tail = divmod(half, LANES)
+
+    pairs = (
+        (saved_in, saved_ref), (weight_in, weight_ref), (cot_in, cot_ref),
+        (coefs_in, coefs_ref), (step_in, step_ref), (reach_in, reach_ref),
+    )
+    loads = [pltpu.make_async_copy(src, dst, load_sem.at[i]) for i, (src, dst) in enumerate(pairs)]
+    for load in loads:
+        load.start()
 
     barrier = pltpu.get_barrier_semaphore()
     for s in range(1, n):
         pl.semaphore_signal(barrier, inc=1, device_id={"lon": lax.rem(me + s, n)}, device_id_type=MESH)
     pl.semaphore_signal(barrier, inc=1, device_id={"lat": other}, device_id_type=MESH)
 
+    acc[...] = jnp.zeros_like(acc)
+    loads[0].wait()
     saved = saved_ref[...].reshape(cells, channels)
     s_t[...] = saved.T.reshape(n, own, cells)
+    loads[1].wait()
+    weight = halves(weight_ref[...])
+    hidden = dot3(halves(saved), weight, ((1,), (0,)))
     pl.semaphore_wait(barrier, n)
 
     def to_peer(src, dst, slot):
@@ -80,8 +96,7 @@
     saved_copy = to_peer(s_t, s_t_peer, 0)
     saved_copy.start()
 
-    weight = halves(weight_ref[...])
-    hidden = dot3(halves(saved), weight, ((1,), (0,)))
+    loads[2].wait()
     pre_grad = cot_ref[...].reshape(cells, channels) * gelu_slope(hidden)
     turned = pre_grad.T
     pg_t[...] = turned.reshape(2, half, cells)
@@ -114,15 +129,23 @@
 
     order = sorted(range(n), key=lambda j: -int(format(j, "b").zfill(bits)[::-1], 2))
     sends = {j: hand_on(j) for j in range(1, n)}
-    mine = halves(pg_t[lat])
     saved_copy.wait_recv()
     pg_copy.wait_recv()
-    theirs = halves(pg_t_peer[...])
-    for j in order:
-        owner = flipped(me, j, n)
-        part[j] = dot3(halves(s_t[owner]), mine, ((1,), (1,))) + dot3(halves(s_t_peer[owner]), theirs, ((1,), (1,)))
-        if j % 2:
-            sends[j].start()
+    columns = halves(jnp.concatenate([pg_t[lat], pg_t_peer[...]], axis=1))
+    for members in (order[: n // 2], order[n // 2 :]):
+        owners = [flipped(me, j, n) for j in members]
+        own_cells = jnp.concatenate([s_t[k] for k in owners], axis=0)
+        peer_cells = jnp.concatenate([s_t_peer[k] for k in owners], axis=0)
+        product = dot3(halves(jnp.concatenate([own_cells, peer_cells], axis=1)), columns, ((1,), (1,)))
+        for at, j in enumerate(members):
+            block = product[at * own : (at + 1) * own]
+            for i in range(full):
+                part[j, i * own : (i + 1) * own] = block[:, i * LANES : (i + 1) * LANES]
+            if tail:
+                rest = block[:, full * LANES :]
+                part[j, full * own :] = jnp.concatenate([rest[: own // 2], rest[own // 2 :]], axis=1)
+            if j % 2:
+                sends[j].start()
 
     def gather(j):
         total = part[j]
@@ -139,7 +162,6 @@
         part[j] = gather(j)
         sends[j].start()
 
-    acc[...] = jnp.zeros_like(acc)
     arrived[me] = cell[me]
     for move in moves:
         move.wait_recv()
@@ -177,7 +199,10 @@
                 summed = term if summed is None else summed + term
             acc[local + offset + 2 * REACH] += summed
 
-    @pl.loop(0, rows)
+    for load in loads[3:]:
+        load.wait()
+
+    @pl.loop(0, rows, unroll=2)
     def _(i):
         scatter(grid_ref[i], lat * rows + i, i)
 
@@ -189,7 +214,13 @@
         scatter(halo[i], lat * rows + local, local)
 
     acc_out[...] = acc[2 * REACH : 2 * REACH + rows]
-    gw_out[...] = gather(0)
+    total = gather(0)
+    for i in range(full):
+        gw_out[:, i * LANES : (i + 1) * LANES] = total[i * own : (i + 1) * own]
+    if tail:
+        packed = total[full * own :]
+        gw_out[: own // 2, full * LANES :] = packed[:, :tail]
+        gw_out[own // 2 :, full * LANES :] = packed[:, tail:]
 
     saved_copy.wait_send()
     pg_copy.wait_send()
@@ -208,24 +239,32 @@
     cells = rows * cols
     f32 = jnp.float32
     vmem = pl.BlockSpec(memory_space=pltpu.VMEM)
-    smem = pl.BlockSpec(memory_space=pltpu.SMEM)
+    anywhere = pl.BlockSpec(memory_space=pl.ANY)
+    packed_rows = own * half // LANES
     acc, grad = pl.pallas_call(
         functools.partial(kernel, n),
         out_shape=(
             jax.ShapeDtypeStruct((rows, n * cols, own), f32),
             jax.ShapeDtypeStruct((own, half), f32),
         ),
-        in_specs=[smem, smem, vmem, vmem, vmem, vmem],
+        in_specs=[anywhere] * 6,
         out_specs=(vmem, vmem),
         scratch_shapes=[
+            pltpu.SMEM(lon_step.shape, lon_step.dtype),
+            pltpu.SMEM(row_reach.shape, row_reach.dtype),
+            pltpu.VMEM(saved.shape, f32),
+            pltpu.VMEM(cotangent.shape, f32),
+            pltpu.VMEM(weight.shape, f32),
+            pltpu.VMEM(coefs.shape, f32),
+            pltpu.SemaphoreType.DMA((6,)),
             pltpu.VMEM((n, own, cells), f32),
             pltpu.VMEM((n, own, cells), f32),
             pltpu.VMEM((2, half, cells), f32),
             pltpu.VMEM((half, cells), f32),
             pltpu.VMEM((n, own, cells), f32),
             pltpu.VMEM((n, own, cells), f32),
-            pltpu.VMEM((n, own, half), f32),
-            pltpu.VMEM((n - 1, own, half), f32),
+            pltpu.VMEM((n, packed_rows, LANES), f32),
+            pltpu.VMEM((n - 1, packed_rows, LANES), f32),
             pltpu.VMEM((rows, n * cols, own), f32),
             pltpu.VMEM((REACH, n * cols, own), f32),
             pltpu.VMEM((rows + 4 * REACH, n * cols, own), f32),
@@ -237,7 +276,7 @@
             pltpu.SemaphoreType.DMA((n - 1,)),
         ],
         compiler_params=pltpu.CompilerParams(
-            collective_id=0, has_side_effects=True, vmem_limit_bytes=40 * 1024 * 1024
+            collective_id=0, has_side_effects=True, vmem_limit_bytes=63 * 1024 * 1024
         ),
     )(lon_step, row_reach, saved, cotangent, weight, coefs)
     scale = 1.0 / math.sqrt(rows * 2 * n * cols)
@@ -341,6 +380,7 @@
         and 4 <= n <= 16
         and n & (n - 1) == 0
         and channels % (16 * n) == 0
+        and channels % LANES == 0
         and (rows * cols) % 128 == 0
         and rows >= REACH
         and n * cols >= MOST_STEP

time: 36.7 us -> 30.6 us (0.83)
  local copies, waits for them, and re-layouts: 6.64 us -> 1.87 us
  Pallas kernels: 28.4 us -> 26.4 us
  other arithmetic: 0.66 us -> 1.56 us
    unnamed x13 -> x1, local copies, waits for them, and re-layouts: 6.64 us -> 1.87 us
    pallas_call x1, Pallas kernels: 28.4 us -> 26.4 us  [kernel_body(): pl.pallas_call(functools.partial(kernel, n), out_shape=(jax.ShapeDtypeStr...]
    mul x1, other arithmetic: 0.66 us -> 1.56 us  [kernel_body(): return (jnp.transpose(acc, (2, 0, 1)), grad * scale)]
where the time goes in v2:
time: 30.6 us; the launch traced here: 30.4 us
  Pallas kernels  26.4 us (86%)
  local copies, waits for them, and re-layouts  1.87 us (6%)
  other arithmetic  1.56 us (5%)
  between operations  0.64 us (2%)
    pallas_call x1, Pallas kernels, kernel_body(): pl.pallas_call(functools.partial(kernel, n), out_shape=(jax.ShapeDtypeStr...  26.4 us
    unnamed x1, local copies, waits for them, and re-layouts  1.87 us
    mul x1, other arithmetic, kernel_body(): return (jnp.transpose(acc, (2, 0, 1)), grad * scale)  1.56 us

profile of v2, /device:TPU:0, one launch (start us, length us, event | category | flops | bytes accessed | tf_op | source)
XLA Modules:
  0.0 30.4 jit_solution(13400667957816861918)
XLA Ops:
  0.6 26.4 %shard_map.77 = (f32[32,32,80]{2,1,0:T(8,128)}, f32[80,320]{1,0:T(8,128)}) custom-call(s32[64]{0:T(128)} %step_in.1, s32[64]{0:T(128)} %reach_in.1, f32[32,4,640]{2,1,0:T(4,128)} %saved_in.1, f32[32,4,640]{2,1,0:T(4,128)} %cot_in.1, f32[640,640]{1,0:T(8,128)} %weight_in.1, f32[27,64,80]{2,1,0:T(8,128)} %coefs_in.1), custom_call_target="tpu_custom_call" | custom-call | tf_op jit(solution)/shard_map/pallas_call | solution.py:244
  27.0 1.6 %broadcast_multiply_fusion = f32[80,320]{1,0:T(8,128)} fusion(f32[80,320]{1,0:T(8,128)} %get-tuple-element.5), kind=kLoop, calls=%fused_computation | loop fusion | flops 25600 | bytes 204800 | tf_op jit(solution)/shard_map/mul | solution.py:283
  28.6 1.9 %copy.9 = f32[80,32,32]{0,2,1:T(8,128)} copy(f32[80,32,32]{0,2,1:T(8,128)} %bitcast.1) | data formatting | bytes 655360

commit v3 on v2

--- a/solution.py
+++ b/solution.py
@@ -214,7 +214,7 @@
         scatter(halo[i], lat * rows + local, local)
 
     acc_out[...] = acc[2 * REACH : 2 * REACH + rows]
-    total = gather(0)
+    total = gather(0) * (1.0 / math.sqrt(2 * rows * all_lon))
     for i in range(full):
         gw_out[:, i * LANES : (i + 1) * LANES] = total[i * own : (i + 1) * own]
     if tail:
@@ -229,6 +229,17 @@
         move.wait_send()
     for j in range(1, n):
         sends[j].wait_send()
+
+
+def write_out(acc_in, grad_in, acc_out, grad_out, sem):
+    copies = [
+        pltpu.make_async_copy(acc_in, acc_out, sem.at[0]),
+        pltpu.make_async_copy(grad_in, grad_out, sem.at[1]),
+    ]
+    for copy in copies:
+        copy.start()
+    for copy in copies:
+        copy.wait()
 
 
 def kernel_body(saved, cotangent, weight, coefs, lon_step, row_reach):
@@ -244,8 +255,8 @@
     acc, grad = pl.pallas_call(
         functools.partial(kernel, n),
         out_shape=(
-            jax.ShapeDtypeStruct((rows, n * cols, own), f32),
-            jax.ShapeDtypeStruct((own, half), f32),
+            pltpu.VMEM((rows, n * cols, own), f32),
+            pltpu.VMEM((own, half), f32),
         ),
         in_specs=[anywhere] * 6,
         out_specs=(vmem, vmem),
@@ -276,11 +287,20 @@
             pltpu.SemaphoreType.DMA((n - 1,)),
         ],
         compiler_params=pltpu.CompilerParams(
-            collective_id=0, has_side_effects=True, vmem_limit_bytes=63 * 1024 * 1024
+            collective_id=0, has_side_effects=True, vmem_limit_bytes=40 * 1024 * 1024
         ),
-    )(lon_step, row_reach, saved, cotangent, weight, coefs)
-    scale = 1.0 / math.sqrt(rows * 2 * n * cols)
-    return jnp.transpose(acc, (2, 0, 1)), grad * scale
+    )(*[
+        pltpu.with_memory_space_constraint(x, pltpu.HBM)
+        for x in (lon_step, row_reach, saved, cotangent, weight, coefs)
+    ])
+    acc, grad = pl.pallas_call(
+        write_out,
+        out_shape=(jax.ShapeDtypeStruct(acc.shape, f32), jax.ShapeDtypeStruct(grad.shape, f32)),
+        in_specs=[anywhere] * 2,
+        out_specs=(anywhere,) * 2,
+        scratch_shapes=[pltpu.SemaphoreType.DMA((2,))],
+    )(acc, grad)
+    return jnp.transpose(acc, (2, 0, 1)), grad
 
 
 def with_halo(x, sides, width):

time: 30.6 us -> 48.5 us (1.58)
  Pallas kernels: 26.4 us -> 46.3 us
  other arithmetic: 1.56 us -> 0 us
    pallas_call x1 -> x2, Pallas kernels: 26.4 us -> 46.3 us  [the longest x1 25.6 us: kernel_body(): pl.pallas_call(functools.partial(kernel, n), out_shape=(pltpu.VMEM((rows,...]
    mul x1 -> x0, other arithmetic: 1.56 us -> none  [kernel_body(): return (jnp.transpose(acc, (2, 0, 1)), grad * scale)]
    unnamed x1 -> x4, local copies, waits for them, and re-layouts: 1.87 us -> 1.42 us
where the time goes in v3:
time: 48.5 us; the launch traced here: 48.3 us
  Pallas kernels  46.3 us (95%)
  local copies, waits for them, and re-layouts  1.42 us (3%)
  between operations  0.65 us (1%)
    pallas_call x1, Pallas kernels, kernel_body(): pl.pallas_call(functools.partial(kernel, n), out_shape=(pltpu.VMEM((rows,...  25.6 us
    pallas_call x1, Pallas kernels, kernel_body(): pl.pallas_call(write_out, out_shape=(jax.ShapeDtypeStruct(acc.shape, f32)...  20.7 us
    unnamed x4, local copies, waits for them, and re-layouts  1.42 us

profile of v3, /device:TPU:0, one launch (start us, length us, event | category | flops | bytes accessed | tf_op | source)
XLA Modules:
  0.0 48.3 jit_solution(4108578652486983347)
XLA Ops:
  0.6 25.6 %shard_map.77 = (f32[32,32,80]{2,1,0:T(8,128)S(1)}, f32[80,320]{1,0:T(8,128)S(1)}) custom-call(s32[64]{0:T(128)} %step_in.1, s32[64]{0:T(128)} %reach_in.1, f32[32,4,640]{2,1,0:T(4,128)} %saved_in.1, f32[32,4,640]{2,1,0:T(4,128)} %cot_in.1, f32[640,640]{1,0:T(8,128)} %weight_in.1, f32[27,64,80]{2,1,0:T(8,128)} %coefs_in.1), custom_call_target="tpu_custom_call" | custom-call | tf_op jit(solution)/shard_map/pallas_call | solution.py:255
  26.2 0.0 copy-start
  26.2 0.8 %copy-done = f32[32,32,80]{2,1,0:T(8,128)} copy-done((f32[32,32,80]{2,1,0:T(8,128)}, f32[32,32,80]{2,1,0:T(8,128)S(1)}, u32[]{:S(2)}) %copy-start) | copy-done | bytes 327704
  27.0 0.0 copy-start.1
  27.0 0.6 %copy-done.1 = f32[80,320]{1,0:T(8,128)} copy-done((f32[80,320]{1,0:T(8,128)}, f32[80,320]{1,0:T(8,128)S(1)}, u32[]{:S(2)}) %copy-start.1) | copy-done | bytes 102424
  27.6 20.7 %shard_map.78 = (f32[32,32,80]{2,1,0:T(8,128)}, f32[80,320]{1,0:T(8,128)}) custom-call(f32[32,32,80]{2,1,0:T(8,128)} %copy-done, f32[80,320]{1,0:T(8,128)} %copy-done.1), custom_call_target="tpu_custom_call" | custom-call | tf_op jit(solution)/shard_map/pallas_call | solution.py:296
Async XLA Ops:
  26.2 0.8 %copy-start = (f32[32,32,80]{2,1,0:T(8,128)}, f32[32,32,80]{2,1,0:T(8,128)S(1)}, u32[]{:S(2)}) copy-start(f32[32,32,80]{2,1,0:T(8,128)S(1)} %get-tuple-element.6.acc_in) | copy-start | bytes 983044
  27.0 0.6 %copy-start.1 = (f32[80,320]{1,0:T(8,128)}, f32[80,320]{1,0:T(8,128)S(1)}, u32[]{:S(2)}) copy-start(f32[80,320]{1,0:T(8,128)S(1)} %get-tuple-element.7.grad_in) | copy-start | bytes 307204

commit v4 on v3

--- a/solution.py
+++ b/solution.py
@@ -51,7 +51,7 @@
     step_in, reach_in, saved_in, cot_in, weight_in, coefs_in,
     acc_out, gw_out,
     step_ref, reach_ref, saved_ref, cot_ref, weight_ref, coefs_ref, load_sem,
-    s_t, s_t_peer, pg_t, pg_t_peer, cell, arrived, part, landed, grid_ref, halo, acc,
+    hid_half, cot_half, s_t, s_t_peer, pg_t, pg_t_peer, cell, arrived, part, landed, grid_ref, halo, acc,
     lat_send, lat_recv, a2a_send, a2a_recv, gw_send, gw_recv,
 ):
     me = lax.axis_index("lon")
@@ -97,24 +97,14 @@
     saved_copy.start()
 
     loads[2].wait()
-    pre_grad = cot_ref[...].reshape(cells, channels) * gelu_slope(hidden)
-    turned = pre_grad.T
-    pg_t[...] = turned.reshape(2, half, cells)
+    cot = cot_ref[...].reshape(cells, channels)
+    for side in range(2):
+        hid_half[side] = hidden[:, side * half : (side + 1) * half]
+        cot_half[side] = cot[:, side * half : (side + 1) * half]
     pg_copy = to_peer(pg_t.at[other], pg_t_peer, 1)
+    pg_t[other] = (cot_half[other] * gelu_slope(hid_half[other])).T
     pg_copy.start()
-
-    cell[...] = dot3(weight, halves(turned), ((1,), (0,))).reshape(n, own, cells)
-
-    def across(s):
-        dest = lax.rem(me + s, n)
-        return pltpu.make_async_remote_copy(
-            src_ref=cell.at[dest], dst_ref=arrived.at[me], send_sem=a2a_send.at[s - 1], recv_sem=a2a_recv.at[s - 1],
-            device_id={"lon": dest}, device_id_type=MESH,
-        )
-
-    moves = [across(s) for s in range(1, n)]
-    for move in moves:
-        move.start()
+    pg_t[lat] = (cot_half[lat] * gelu_slope(hid_half[lat])).T
 
     def slot_of(stage, j):
         return n - (n >> stage) + j // (2 << stage)
@@ -132,7 +122,8 @@
     saved_copy.wait_recv()
     pg_copy.wait_recv()
     columns = halves(jnp.concatenate([pg_t[lat], pg_t_peer[...]], axis=1))
-    for members in (order[: n // 2], order[n // 2 :]):
+
+    def multiply(members):
         owners = [flipped(me, j, n) for j in members]
         own_cells = jnp.concatenate([s_t[k] for k in owners], axis=0)
         peer_cells = jnp.concatenate([s_t_peer[k] for k in owners], axis=0)
@@ -144,8 +135,27 @@
             if tail:
                 rest = block[:, full * LANES :]
                 part[j, full * own :] = jnp.concatenate([rest[: own // 2], rest[own // 2 :]], axis=1)
-            if j % 2:
-                sends[j].start()
+
+    odd = order[: n // 2]
+    multiply(odd)
+    sends[odd[0]].start()
+
+    turned = halves(pg_t[...].reshape(channels, cells))
+    cell[...] = dot3(weight, turned, ((1,), (0,))).reshape(n, own, cells)
+
+    def across(s):
+        dest = lax.rem(me + s, n)
+        return pltpu.make_async_remote_copy(
+            src_ref=cell.at[dest], dst_ref=arrived.at[me], send_sem=a2a_send.at[s - 1], recv_sem=a2a_recv.at[s - 1],
+            device_id={"lon": dest}, device_id_type=MESH,
+        )
+
+    moves = [across(s) for s in range(1, n)]
+    for move in moves:
+        move.start()
+    for j in odd[1:]:
+        sends[j].start()
+    multiply(order[n // 2 :])
 
     def gather(j):
         total = part[j]
@@ -268,6 +278,8 @@
             pltpu.VMEM(weight.shape, f32),
             pltpu.VMEM(coefs.shape, f32),
             pltpu.SemaphoreType.DMA((6,)),
+            pltpu.VMEM((2, cells, half), f32),
+            pltpu.VMEM((2, cells, half), f32),
             pltpu.VMEM((n, own, cells), f32),
             pltpu.VMEM((n, own, cells), f32),
             pltpu.VMEM((2, half, cells), f32),
@@ -296,7 +308,7 @@
     acc, grad = pl.pallas_call(
         write_out,
         out_shape=(jax.ShapeDtypeStruct(acc.shape, f32), jax.ShapeDtypeStruct(grad.shape, f32)),
-        in_specs=[anywhere] * 2,
+        in_specs=[vmem] * 2,
         out_specs=(anywhere,) * 2,
         scratch_shapes=[pltpu.SemaphoreType.DMA((2,))],
     )(acc, grad)

time: 48.5 us -> 30.9 us (0.64)
  Pallas kernels: 46.3 us -> 28.7 us
    pallas_call x1, Pallas kernels: 20.7 us -> 1.9 us  [kernel_body(): pl.pallas_call(write_out, out_shape=(jax.ShapeDtypeStruct(acc.shape, f32)...]
    pallas_call x1, Pallas kernels: 25.6 us -> 26.8 us  [kernel_body(): pl.pallas_call(functools.partial(kernel, n), out_shape=(pltpu.VMEM((rows,...]
where the time goes in v4:
time: 30.9 us; the launch traced here: 30.8 us
  Pallas kernels  28.7 us (93%)
  local copies, waits for them, and re-layouts  1.42 us (5%)
  between operations  0.65 us (2%)
    pallas_call x1, Pallas kernels, kernel_body(): pl.pallas_call(functools.partial(kernel, n), out_shape=(pltpu.VMEM((rows,...  26.8 us
    pallas_call x1, Pallas kernels, kernel_body(): pl.pallas_call(write_out, out_shape=(jax.ShapeDtypeStruct(acc.shape, f32)...  1.9 us
    unnamed x4, local copies, waits for them, and re-layouts  1.42 us

profile of v4, /device:TPU:0, one launch (start us, length us, event | category | flops | bytes accessed | tf_op | source)
XLA Modules:
  0.0 30.8 jit_solution(13837500331848510362)
XLA Ops:
  0.6 26.8 %shard_map.77 = (f32[32,32,80]{2,1,0:T(8,128)S(1)}, f32[80,320]{1,0:T(8,128)S(1)}) custom-call(s32[64]{0:T(128)} %step_in.1, s32[64]{0:T(128)} %reach_in.1, f32[32,4,640]{2,1,0:T(4,128)} %saved_in.1, f32[32,4,640]{2,1,0:T(4,128)} %cot_in.1, f32[640,640]{1,0:T(8,128)} %weight_in.1, f32[27,64,80]{2,1,0:T(8,128)} %coefs_in.1), custom_call_target="tpu_custom_call" | custom-call | tf_op jit(solution)/shard_map/pallas_call | solution.py:265
  27.4 0.0 copy-start
  27.5 0.8 %copy-done = f32[32,32,80]{2,1,0:T(8,128)} copy-done((f32[32,32,80]{2,1,0:T(8,128)}, f32[32,32,80]{2,1,0:T(8,128)S(1)}, u32[]{:S(2)}) %copy-start) | copy-done | bytes 327704
  28.2 0.0 copy-start.1
  28.2 0.6 %copy-done.1 = f32[80,320]{1,0:T(8,128)} copy-done((f32[80,320]{1,0:T(8,128)}, f32[80,320]{1,0:T(8,128)S(1)}, u32[]{:S(2)}) %copy-start.1) | copy-done | bytes 102424
  28.9 1.9 %shard_map.78 = (f32[32,32,80]{2,1,0:T(8,128)}, f32[80,320]{1,0:T(8,128)}) custom-call(f32[32,32,80]{2,1,0:T(8,128)} %copy-done, f32[80,320]{1,0:T(8,128)} %copy-done.1), custom_call_target="tpu_custom_call" | custom-call | tf_op jit(solution)/shard_map/pallas_call | solution.py:308
Async XLA Ops:
  27.4 0.8 %copy-start = (f32[32,32,80]{2,1,0:T(8,128)}, f32[32,32,80]{2,1,0:T(8,128)S(1)}, u32[]{:S(2)}) copy-start(f32[32,32,80]{2,1,0:T(8,128)S(1)} %get-tuple-element.6.acc_in) | copy-start | bytes 983044
  28.2 0.6 %copy-start.1 = (f32[80,320]{1,0:T(8,128)}, f32[80,320]{1,0:T(8,128)S(1)}, u32[]{:S(2)}) copy-start(f32[80,320]{1,0:T(8,128)S(1)} %get-tuple-element.7.grad_in) | copy-start | bytes 307204

commit v5 on v3

--- a/solution.py
+++ b/solution.py
@@ -11,6 +11,8 @@
 MESH = pl.DeviceIdType.MESH
 REACH = 4
 MOST_STEP = 8
+WEIGHT_PARTS = 4
+SUBLANES = 8
 LANES = 128
 
 
@@ -51,7 +53,7 @@
     step_in, reach_in, saved_in, cot_in, weight_in, coefs_in,
     acc_out, gw_out,
     step_ref, reach_ref, saved_ref, cot_ref, weight_ref, coefs_ref, load_sem,
-    s_t, s_t_peer, pg_t, pg_t_peer, cell, arrived, part, landed, grid_ref, halo, acc,
+    s_t, s_t_peer, pg_t, pg_t_peer, cell, arrived, part, landed, grid_ref, halo, taps, rolled,
     lat_send, lat_recv, a2a_send, a2a_recv, gw_send, gw_recv,
 ):
     me = lax.axis_index("lon")
@@ -65,12 +67,13 @@
     bits = n.bit_length() - 1
     full, tail = divmod(half, LANES)
 
-    pairs = (
-        (saved_in, saved_ref), (weight_in, weight_ref), (cot_in, cot_ref),
-        (coefs_in, coefs_ref), (step_in, step_ref), (reach_in, reach_ref),
-    )
+    slab = channels // WEIGHT_PARTS
+    pairs = [(saved_in, saved_ref)]
+    pairs += [(weight_in.at[pl.ds(i * slab, slab)], weight_ref.at[pl.ds(i * slab, slab)]) for i in range(WEIGHT_PARTS)]
+    pairs += [(cot_in, cot_ref), (coefs_in, coefs_ref), (step_in, step_ref), (reach_in, reach_ref)]
     loads = [pltpu.make_async_copy(src, dst, load_sem.at[i]) for i, (src, dst) in enumerate(pairs)]
-    for load in loads:
+    late = WEIGHT_PARTS + 2
+    for load in loads[:late]:
         load.start()
 
     barrier = pltpu.get_barrier_semaphore()
@@ -78,11 +81,13 @@
         pl.semaphore_signal(barrier, inc=1, device_id={"lon": lax.rem(me + s, n)}, device_id_type=MESH)
     pl.semaphore_signal(barrier, inc=1, device_id={"lat": other}, device_id_type=MESH)
 
-    acc[...] = jnp.zeros_like(acc)
     loads[0].wait()
     saved = saved_ref[...].reshape(cells, channels)
     s_t[...] = saved.T.reshape(n, own, cells)
-    loads[1].wait()
+    for load in loads[1 : 1 + WEIGHT_PARTS]:
+        load.wait()
+    for load in loads[late:]:
+        load.start()
     weight = halves(weight_ref[...])
     hidden = dot3(halves(saved), weight, ((1,), (0,)))
     pl.semaphore_wait(barrier, n)
@@ -96,7 +101,7 @@
     saved_copy = to_peer(s_t, s_t_peer, 0)
     saved_copy.start()
 
-    loads[2].wait()
+    loads[1 + WEIGHT_PARTS].wait()
     pre_grad = cot_ref[...].reshape(cells, channels) * gelu_slope(hidden)
     turned = pre_grad.T
     pg_t[...] = turned.reshape(2, half, cells)
@@ -155,6 +160,28 @@
             total = total + landed[slot_of(stage, j)]
         return total
 
+    for load in loads[late:]:
+        load.wait()
+
+    def taps_of(place):
+        row = lat * rows + place - REACH
+        for tap in range(3 * (2 * REACH + 1)):
+            live = jnp.where(abs(tap // 3 - REACH) <= reach_ref[row], 1.0, 0.0).astype(jnp.float32)
+            taps[place, tap] = jnp.broadcast_to(coefs_ref[tap, pl.ds(row, 1), :] * live, (SUBLANES, own))
+
+    beyond = (rows + REACH) * lat
+    halo_at = (rows + REACH) * other
+
+    @pl.loop(0, REACH)
+    def _(i):
+        taps[beyond + i] = jnp.zeros(taps.shape[1:], jnp.float32)
+        rolled[beyond + i] = jnp.zeros(rolled.shape[1:], jnp.float32)
+        taps_of(halo_at + i)
+
+    @pl.loop(0, rows)
+    def _(i):
+        taps_of(REACH + i)
+
     later = [j for j in order if j % 2 == 0 and j]
     first = [j for j in later if j % 4]
     rest = [j for j in later if not j % 4]
@@ -179,9 +206,8 @@
         part[j] = gather(j)
         sends[j].start()
 
-    def scatter(values, row, local):
-        step = jnp.full(values.shape, step_ref[row], jnp.int32)
-        reach = reach_ref[row]
+    def roll_row(values, place):
+        step = jnp.full(values.shape, step_ref[lat * rows + place - REACH], jnp.int32)
         up = values
         down = values
         bit = 1
@@ -190,30 +216,43 @@
             up = jnp.where(chosen, jnp.roll(up, bit, axis=0), up)
             down = jnp.where(chosen, jnp.roll(down, -bit, axis=0), down)
             bit *= 2
-        rolled = (down, values, up)
-        for offset in range(-REACH, REACH + 1):
-            live = jnp.where(abs(offset) <= reach, 1.0, 0.0).astype(jnp.float32)
-            summed = None
-            for side in range(3):
-                term = coefs_ref[3 * (offset + REACH) + side, pl.ds(row, 1), :] * live * rolled[side]
-                summed = term if summed is None else summed + term
-            acc[local + offset + 2 * REACH] += summed
-
-    for load in loads[3:]:
-        load.wait()
+        rolled[place, 0] = down
+        rolled[place, 1] = values
+        rolled[place, 2] = up
+
+    def sum_rows(group):
+        base = group * REACH
+        sums = [None] * REACH
+        for away in range(3 * REACH):
+            sources = [rolled[base + away, side].reshape(all_lon // SUBLANES, SUBLANES, own) for side in range(3)]
+            for q in range(REACH):
+                offset = q + REACH - away
+                if abs(offset) > REACH:
+                    continue
+                for side in range(3):
+                    term = taps[base + away, 3 * (offset + REACH) + side][None] * sources[side]
+                    sums[q] = term if sums[q] is None else sums[q] + term
+        for q in range(REACH):
+            acc_out[base + q] = sums[q].reshape(all_lon, own)
 
     @pl.loop(0, rows, unroll=2)
     def _(i):
-        scatter(grid_ref[i], lat * rows + i, i)
+        roll_row(grid_ref[i], REACH + i)
+
+    groups = rows // REACH
+
+    @pl.loop(0, groups - 1)
+    def _(i):
+        sum_rows(lax.rem(i + lat, groups))
 
     halo_copy.wait_recv()
 
     @pl.loop(0, REACH)
     def _(i):
-        local = rows * other - REACH * lat + i
-        scatter(halo[i], lat * rows + local, local)
-
-    acc_out[...] = acc[2 * REACH : 2 * REACH + rows]
+        roll_row(halo[i], halo_at + i)
+
+    sum_rows(lax.rem(groups - 1 + lat, groups))
+
     total = gather(0) * (1.0 / math.sqrt(2 * rows * all_lon))
     for i in range(full):
         gw_out[:, i * LANES : (i + 1) * LANES] = total[i * own : (i + 1) * own]
@@ -229,17 +268,6 @@
         move.wait_send()
     for j in range(1, n):
         sends[j].wait_send()
-
-
-def write_out(acc_in, grad_in, acc_out, grad_out, sem):
-    copies = [
-        pltpu.make_async_copy(acc_in, acc_out, sem.at[0]),
-        pltpu.make_async_copy(grad_in, grad_out, sem.at[1]),
-    ]
-    for copy in copies:
-        copy.start()
-    for copy in copies:
-        copy.wait()
 
 
 def kernel_body(saved, cotangent, weight, coefs, lon_step, row_reach):
@@ -267,7 +295,7 @@
             pltpu.VMEM(cotangent.shape, f32),
             pltpu.VMEM(weight.shape, f32),
             pltpu.VMEM(coefs.shape, f32),
-            pltpu.SemaphoreType.DMA((6,)),
+            pltpu.SemaphoreType.DMA((WEIGHT_PARTS + 5,)),
             pltpu.VMEM((n, own, cells), f32),
             pltpu.VMEM((n, own, cells), f32),
             pltpu.VMEM((2, half, cells), f32),
@@ -278,7 +306,8 @@
             pltpu.VMEM((n - 1, packed_rows, LANES), f32),
             pltpu.VMEM((rows, n * cols, own), f32),
             pltpu.VMEM((REACH, n * cols, own), f32),
-            pltpu.VMEM((rows + 4 * REACH, n * cols, own), f32),
+            pltpu.VMEM((rows + 2 * REACH, coefs.shape[0], SUBLANES, own), f32),
+            pltpu.VMEM((rows + 2 * REACH, 3, n * cols, own), f32),
             pltpu.SemaphoreType.DMA((3,)),
             pltpu.SemaphoreType.DMA((3,)),
             pltpu.SemaphoreType.DMA((n - 1,)),
@@ -293,13 +322,6 @@
         pltpu.with_memory_space_constraint(x, pltpu.HBM)
         for x in (lon_step, row_reach, saved, cotangent, weight, coefs)
     ])
-    acc, grad = pl.pallas_call(
-        write_out,
-        out_shape=(jax.ShapeDtypeStruct(acc.shape, f32), jax.ShapeDtypeStruct(grad.shape, f32)),
-        in_specs=[anywhere] * 2,
-        out_specs=(anywhere,) * 2,
-        scratch_shapes=[pltpu.SemaphoreType.DMA((2,))],
-    )(acc, grad)
     return jnp.transpose(acc, (2, 0, 1)), grad
 
 
@@ -402,8 +424,11 @@
         and channels % (16 * n) == 0
         and channels % LANES == 0
         and (rows * cols) % 128 == 0
-        and rows >= REACH
-        and n * cols >= MOST_STEP
+        and rows % REACH == 0
+        and rows >= 2 * REACH
+        and n * cols % SUBLANES == 0
+        and n * cols >= 2 * MOST_STEP
+        and channels % (SUBLANES * WEIGHT_PARTS) == 0
     )
     run = kernel_body if fits else collective_body
     return run(saved, cotangent, weight, coefs, lon_step, row_reach)

time: 48.5 us -> 27.8 us (0.57)
  Pallas kernels: 46.3 us -> 25.6 us
    pallas_call x1 -> x0, Pallas kernels: 20.7 us -> none  [kernel_body(): pl.pallas_call(write_out, out_shape=(jax.ShapeDtypeStruct(acc.shape, f32)...]
    unnamed x4 -> x2, local copies, waits for them, and re-layouts: 1.42 us -> 1.44 us
where the time goes in v5:
time: 27.8 us; the launch traced here: 27.7 us
  Pallas kernels  25.6 us (92%)
  local copies, waits for them, and re-layouts  1.44 us (5%)
  between operations  0.64 us (2%)
    pallas_call x1, Pallas kernels, kernel_body(): pl.pallas_call(functools.partial(kernel, n), out_shape=(pltpu.VMEM((rows,...  25.6 us
    unnamed x2, local copies, waits for them, and re-layouts  1.44 us

profile of v5, /device:TPU:0, one launch (start us, length us, event | category | flops | bytes accessed | tf_op | source)
XLA Modules:
  0.0 27.7 jit_solution(7427614928265770862)
XLA Ops:
  0.6 25.6 %shard_map.77 = (f32[32,32,80]{2,1,0:T(8,128)S(1)}, f32[80,320]{1,0:T(8,128)S(1)}) custom-call(s32[64]{0:T(128)} %step_in.1, s32[64]{0:T(128)} %reach_in.1, f32[32,4,640]{2,1,0:T(4,128)} %saved_in.1, f32[32,4,640]{2,1,0:T(4,128)} %cot_in.1, f32[640,640]{1,0:T(8,128)} %weight_in.1, f32[27,64,80]{2,1,0:T(8,128)} %coefs_in.1), custom_call_target="tpu_custom_call" | custom-call | tf_op jit(solution)/shard_map/pallas_call | solution.py:283
  26.2 0.8 %copy.10 = f32[80,32,32]{0,2,1:T(8,128)} copy(f32[80,32,32]{0,2,1:T(8,128)S(1)} %bitcast.1) | data formatting | bytes 655360
  27.0 0.6 %copy.11 = f32[80,320]{1,0:T(8,128)} copy(f32[80,320]{1,0:T(8,128)S(1)} %get-tuple-element.7) | data formatting | bytes 204800

commit v6 on v5

--- a/solution.py
+++ b/solution.py
@@ -182,10 +182,7 @@
     def _(i):
         taps_of(REACH + i)
 
-    later = [j for j in order if j % 2 == 0 and j]
-    first = [j for j in later if j % 4]
-    rest = [j for j in later if not j % 4]
-    for j in first:
+    for j in order[n // 2 : -1]:
         part[j] = gather(j)
         sends[j].start()
 
@@ -201,10 +198,6 @@
         device_id={"lat": other}, device_id_type=MESH,
     )
     halo_copy.start()
-
-    for j in rest:
-        part[j] = gather(j)
-        sends[j].start()
 
     def roll_row(values, place):
         step = jnp.full(values.shape, step_ref[lat * rows + place - REACH], jnp.int32)

time: 27.8 us -> 27.8 us (level)
  no operation moved by 1% of the time
where the time goes in v6:
time: 27.8 us; the launch traced here: 27.7 us
  Pallas kernels  25.6 us (92%)
  local copies, waits for them, and re-layouts  1.44 us (5%)
  between operations  0.64 us (2%)
    pallas_call x1, Pallas kernels, kernel_body(): pl.pallas_call(functools.partial(kernel, n), out_shape=(pltpu.VMEM((rows,...  25.6 us
    unnamed x2, local copies, waits for them, and re-layouts  1.44 us

profile of v6, /device:TPU:0, one launch (start us, length us, event | category | flops | bytes accessed | tf_op | source)
XLA Modules:
  0.0 27.7 jit_solution(6590432326635258579)
XLA Ops:
  0.6 25.6 %shard_map.77 = (f32[32,32,80]{2,1,0:T(8,128)S(1)}, f32[80,320]{1,0:T(8,128)S(1)}) custom-call(s32[64]{0:T(128)} %step_in.1, s32[64]{0:T(128)} %reach_in.1, f32[32,4,640]{2,1,0:T(4,128)} %saved_in.1, f32[32,4,640]{2,1,0:T(4,128)} %cot_in.1, f32[640,640]{1,0:T(8,128)} %weight_in.1, f32[27,64,80]{2,1,0:T(8,128)} %coefs_in.1), custom_call_target="tpu_custom_call" | custom-call | tf_op jit(solution)/shard_map/pallas_call | solution.py:276
  26.2 0.8 %copy.10 = f32[80,32,32]{0,2,1:T(8,128)} copy(f32[80,32,32]{0,2,1:T(8,128)S(1)} %bitcast.1) | data formatting | bytes 655360
  27.0 0.6 %copy.11 = f32[80,320]{1,0:T(8,128)} copy(f32[80,320]{1,0:T(8,128)S(1)} %get-tuple-element.7) | data formatting | bytes 204800

commit v7 on v6

--- a/solution.py
+++ b/solution.py
@@ -53,7 +53,7 @@
     step_in, reach_in, saved_in, cot_in, weight_in, coefs_in,
     acc_out, gw_out,
     step_ref, reach_ref, saved_ref, cot_ref, weight_ref, coefs_ref, load_sem,
-    s_t, s_t_peer, pg_t, pg_t_peer, cell, arrived, part, landed, grid_ref, halo, taps, rolled,
+    s_t, s_t_peer, pg_t, pg_t_peer, cell, arrived, part, landed, weight_high, weight_low, slots, edge, halo, taps, rolled,
     lat_send, lat_recv, a2a_send, a2a_recv, gw_send, gw_recv,
 ):
     me = lax.axis_index("lon")
@@ -89,6 +89,8 @@
     for load in loads[late:]:
         load.start()
     weight = halves(weight_ref[...])
+    weight_high[...] = weight[0].reshape(n, own, channels)
+    weight_low[...] = weight[1].reshape(n, own, channels)
     hidden = dot3(halves(saved), weight, ((1,), (0,)))
     pl.semaphore_wait(barrier, n)
 
@@ -108,8 +110,6 @@
     pg_copy = to_peer(pg_t.at[other], pg_t_peer, 1)
     pg_copy.start()
 
-    cell[...] = dot3(weight, halves(turned), ((1,), (0,))).reshape(n, own, cells)
-
     def across(s):
         dest = lax.rem(me + s, n)
         return pltpu.make_async_remote_copy(
@@ -117,9 +117,17 @@
             device_id={"lon": dest}, device_id_type=MESH,
         )
 
-    moves = [across(s) for s in range(1, n)]
-    for move in moves:
-        move.start()
+    moves = {s: across(s) for s in range(1, n)}
+    spans = list(range(n // 4, 3 * n // 4)), list(range(3 * n // 4, n)) + list(range(n // 4))
+    right = halves(turned)
+    for span in spans:
+        owners = [lax.rem(me + s, n) for s in span]
+        left = tuple(jnp.concatenate([ref[k] for k in owners], axis=0) for ref in (weight_high, weight_low))
+        made = dot3(left, right, ((1,), (0,)))
+        for at, s in enumerate(span):
+            cell[owners[at]] = made[at * own : (at + 1) * own]
+            if s:
+                moves[s].start()
 
     def slot_of(stage, j):
         return n - (n >> stage) + j // (2 << stage)
@@ -182,22 +190,38 @@
     def _(i):
         taps_of(REACH + i)
 
-    for j in order[n // 2 : -1]:
+    chained = order[n // 2]
+    part[chained] = gather(chained)
+    sends[chained].start()
+
+    slots[me] = cell[me].T
+    for s in range(1, n):
+        moves[s].wait_recv()
+        source = lax.rem(me - s + n, n)
+        slots[source] = arrived[source].T
+
+    def row_pair(pair):
+        at = pl.ds(pl.multiple_of(pair * SUBLANES, SUBLANES), SUBLANES)
+        low = lax.broadcasted_iota(jnp.int32, (SUBLANES, own), 0) < cols
+        even, odd = [], []
+        for k in range(0, n, 2):
+            a, b = slots[k, at, :], slots[k + 1, at, :]
+            even.append(jnp.where(low, a, jnp.roll(b, cols, axis=0)))
+            odd.append(jnp.where(low, jnp.roll(a, cols, axis=0), b))
+        return jnp.concatenate(even, axis=0), jnp.concatenate(odd, axis=0)
+
+    for i in range(0, REACH, 2):
+        edge[i], edge[i + 1] = row_pair((rows - REACH) // 2 * other + i // 2)
+
+    halo_copy = pltpu.make_async_remote_copy(
+        src_ref=edge, dst_ref=halo, send_sem=lat_send.at[2], recv_sem=lat_recv.at[2],
+        device_id={"lat": other}, device_id_type=MESH,
+    )
+    halo_copy.start()
+
+    for j in order[n // 2 + 1 : -1]:
         part[j] = gather(j)
         sends[j].start()
-
-    arrived[me] = cell[me]
-    for move in moves:
-        move.wait_recv()
-    for source in range(n):
-        grid_ref[:, source * cols : (source + 1) * cols, :] = arrived[source].T.reshape(rows, cols, own)
-
-    halo_copy = pltpu.make_async_remote_copy(
-        src_ref=grid_ref.at[pl.ds((rows - REACH) * other, REACH)], dst_ref=halo,
-        send_sem=lat_send.at[2], recv_sem=lat_recv.at[2],
-        device_id={"lat": other}, device_id_type=MESH,
-    )
-    halo_copy.start()
 
     def roll_row(values, place):
         step = jnp.full(values.shape, step_ref[lat * rows + place - REACH], jnp.int32)
@@ -228,9 +252,11 @@
         for q in range(REACH):
             acc_out[base + q] = sums[q].reshape(all_lon, own)
 
-    @pl.loop(0, rows, unroll=2)
-    def _(i):
-        roll_row(grid_ref[i], REACH + i)
+    @pl.loop(0, rows // 2)
+    def _(pair):
+        even, odd = row_pair(pair)
+        roll_row(even, REACH + 2 * pair)
+        roll_row(odd, REACH + 2 * pair + 1)
 
     groups = rows // REACH
 
@@ -257,8 +283,8 @@
     saved_copy.wait_send()
     pg_copy.wait_send()
     halo_copy.wait_send()
-    for move in moves:
-        move.wait_send()
+    for s in range(1, n):
+        moves[s].wait_send()
     for j in range(1, n):
         sends[j].wait_send()
 
@@ -297,7 +323,10 @@
             pltpu.VMEM((n, own, cells), f32),
             pltpu.VMEM((n, packed_rows, LANES), f32),
             pltpu.VMEM((n - 1, packed_rows, LANES), f32),
-            pltpu.VMEM((rows, n * cols, own), f32),
+            pltpu.VMEM((n, own, channels), jnp.bfloat16),
+            pltpu.VMEM((n, own, channels), jnp.bfloat16),
+            pltpu.VMEM((n, cells, own), f32),
+            pltpu.VMEM((REACH, n * cols, own), f32),
             pltpu.VMEM((REACH, n * cols, own), f32),
             pltpu.VMEM((rows + 2 * REACH, coefs.shape[0], SUBLANES, own), f32),
             pltpu.VMEM((rows + 2 * REACH, 3, n * cols, own), f32),
@@ -419,7 +448,7 @@
         and (rows * cols) % 128 == 0
         and rows % REACH == 0
         and rows >= 2 * REACH
-        and n * cols % SUBLANES == 0
+        and 2 * cols == SUBLANES
         and n * cols >= 2 * MOST_STEP
         and channels % (SUBLANES * WEIGHT_PARTS) == 0
     )

time: 27.8 us -> 28 us (level)
  no operation moved by 1% of the time
where the time goes in v7:
time: 28 us; the launch traced here: 27.8 us
  Pallas kernels  25.8 us (92%)
  local copies, waits for them, and re-layouts  1.44 us (5%)
  between operations  0.64 us (2%)
    pallas_call x1, Pallas kernels, kernel_body(): pl.pallas_call(functools.partial(kernel, n), out_shape=(pltpu.VMEM((rows,...  25.8 us
    unnamed x2, local copies, waits for them, and re-layouts  1.44 us

profile of v7, /device:TPU:0, one launch (start us, length us, event | category | flops | bytes accessed | tf_op | source)
XLA Modules:
  0.0 27.8 jit_solution(14740192208353786732)
XLA Ops:
  0.6 25.8 %shard_map.77 = (f32[32,32,80]{2,1,0:T(8,128)S(1)}, f32[80,320]{1,0:T(8,128)S(1)}) custom-call(s32[64]{0:T(128)} %step_in.1, s32[64]{0:T(128)} %reach_in.1, f32[32,4,640]{2,1,0:T(4,128)} %saved_in.1, f32[32,4,640]{2,1,0:T(4,128)} %cot_in.1, f32[640,640]{1,0:T(8,128)} %weight_in.1, f32[27,64,80]{2,1,0:T(8,128)} %coefs_in.1), custom_call_target="tpu_custom_call" | custom-call | tf_op jit(solution)/shard_map/pallas_call | solution.py:302
  26.4 0.8 %copy.10 = f32[80,32,32]{0,2,1:T(8,128)} copy(f32[80,32,32]{0,2,1:T(8,128)S(1)} %bitcast.1) | data formatting | bytes 655360
  27.2 0.6 %copy.11 = f32[80,320]{1,0:T(8,128)} copy(f32[80,320]{1,0:T(8,128)S(1)} %get-tuple-element.7) | data formatting | bytes 204800

commit v8 on v7

--- a/solution.py
+++ b/solution.py
@@ -157,7 +157,7 @@
             if tail:
                 rest = block[:, full * LANES :]
                 part[j, full * own :] = jnp.concatenate([rest[: own // 2], rest[own // 2 :]], axis=1)
-            if j % 2:
+            if at == 0 and j % 2:
                 sends[j].start()
 
     def gather(j):
@@ -190,9 +190,11 @@
     def _(i):
         taps_of(REACH + i)
 
-    chained = order[n // 2]
-    part[chained] = gather(chained)
-    sends[chained].start()
+    for before, odd, even in zip(order, order[1 : n // 2], order[n // 2 : -1]):
+        sends[before].wait_send()
+        sends[odd].start()
+        part[even] = gather(even)
+        sends[even].start()
 
     slots[me] = cell[me].T
     for s in range(1, n):
@@ -218,10 +220,6 @@
         device_id={"lat": other}, device_id_type=MESH,
     )
     halo_copy.start()
-
-    for j in order[n // 2 + 1 : -1]:
-        part[j] = gather(j)
-        sends[j].start()
 
     def roll_row(values, place):
         step = jnp.full(values.shape, step_ref[lat * rows + place - REACH], jnp.int32)
@@ -285,7 +283,7 @@
     halo_copy.wait_send()
     for s in range(1, n):
         moves[s].wait_send()
-    for j in range(1, n):
+    for j in order[n // 2 - 1 : -1]:
         sends[j].wait_send()
 
 

time: 28 us -> 26.4 us (0.943)
  Pallas kernels: 25.8 us -> 24.2 us
    pallas_call x1, Pallas kernels: 25.8 us -> 24.2 us  [kernel_body(): pl.pallas_call(functools.partial(kernel, n), out_shape=(pltpu.VMEM((rows,...]
where the time goes in v8:
time: 26.4 us; the launch traced here: 26.3 us
  Pallas kernels  24.2 us (92%)
  local copies, waits for them, and re-layouts  1.44 us (5%)
  between operations  0.64 us (2%)
    pallas_call x1, Pallas kernels, kernel_body(): pl.pallas_call(functools.partial(kernel, n), out_shape=(pltpu.VMEM((rows,...  24.2 us
    unnamed x2, local copies, waits for them, and re-layouts  1.44 us

profile of v8, /device:TPU:0, one launch (start us, length us, event | category | flops | bytes accessed | tf_op | source)
XLA Modules:
  0.0 26.3 jit_solution(3956865380490032990)
XLA Ops:
  0.6 24.2 %shard_map.77 = (f32[32,32,80]{2,1,0:T(8,128)S(1)}, f32[80,320]{1,0:T(8,128)S(1)}) custom-call(s32[64]{0:T(128)} %step_in.1, s32[64]{0:T(128)} %reach_in.1, f32[32,4,640]{2,1,0:T(4,128)} %saved_in.1, f32[32,4,640]{2,1,0:T(4,128)} %cot_in.1, f32[640,640]{1,0:T(8,128)} %weight_in.1, f32[27,64,80]{2,1,0:T(8,128)} %coefs_in.1), custom_call_target="tpu_custom_call" | custom-call | tf_op jit(solution)/shard_map/pallas_call | solution.py:300
  24.8 0.8 %copy.10 = f32[80,32,32]{0,2,1:T(8,128)} copy(f32[80,32,32]{0,2,1:T(8,128)S(1)} %bitcast.1) | data formatting | bytes 655360
  25.6 0.6 %copy.11 = f32[80,320]{1,0:T(8,128)} copy(f32[80,320]{1,0:T(8,128)S(1)} %get-tuple-element.7) | data formatting | bytes 204800

commit v9 on v8

--- a/solution.py
+++ b/solution.py
@@ -13,6 +13,7 @@
 MOST_STEP = 8
 WEIGHT_PARTS = 4
 SUBLANES = 8
+WINDOW = 2
 LANES = 128
 
 
@@ -157,7 +158,7 @@
             if tail:
                 rest = block[:, full * LANES :]
                 part[j, full * own :] = jnp.concatenate([rest[: own // 2], rest[own // 2 :]], axis=1)
-            if at == 0 and j % 2:
+            if at < WINDOW and j % 2:
                 sends[j].start()
 
     def gather(j):
@@ -190,9 +191,10 @@
     def _(i):
         taps_of(REACH + i)
 
-    for before, odd, even in zip(order, order[1 : n // 2], order[n // 2 : -1]):
-        sends[before].wait_send()
-        sends[odd].start()
+    for at, even in enumerate(order[n // 2 : -1]):
+        if at + WINDOW < n // 2:
+            sends[order[at]].wait_send()
+            sends[order[at + WINDOW]].start()
         part[even] = gather(even)
         sends[even].start()
 
@@ -283,8 +285,19 @@
     halo_copy.wait_send()
     for s in range(1, n):
         moves[s].wait_send()
-    for j in order[n // 2 - 1 : -1]:
+    for j in order[n // 2 - WINDOW : -1]:
         sends[j].wait_send()
+
+
+def write_out(acc_in, grad_in, acc_out, grad_out, sem):
+    copies = [
+        pltpu.make_async_copy(acc_in, acc_out, sem.at[0]),
+        pltpu.make_async_copy(grad_in, grad_out, sem.at[1]),
+    ]
+    for copy in copies:
+        copy.start()
+    for copy in copies:
+        copy.wait()
 
 
 def kernel_body(saved, cotangent, weight, coefs, lon_step, row_reach):
@@ -342,6 +355,13 @@
         pltpu.with_memory_space_constraint(x, pltpu.HBM)
         for x in (lon_step, row_reach, saved, cotangent, weight, coefs)
     ])
+    acc, grad = pl.pallas_call(
+        write_out,
+        out_shape=(jax.ShapeDtypeStruct(acc.shape, f32), jax.ShapeDtypeStruct(grad.shape, f32)),
+        in_specs=[vmem] * 2,
+        out_specs=(anywhere,) * 2,
+        scratch_shapes=[pltpu.SemaphoreType.DMA((2,))],
+    )(*[pltpu.with_memory_space_constraint(x, pltpu.VMEM) for x in (acc, grad)])
     return jnp.transpose(acc, (2, 0, 1)), grad
 
 

time: 26.4 us -> 27.4 us (1.038)
  Pallas kernels: 24.2 us -> 26.6 us
  local copies, waits for them, and re-layouts: 1.44 us -> 0 us
    pallas_call x1, Pallas kernels: 24.2 us -> 25.8 us  [kernel_body(): pl.pallas_call(functools.partial(kernel, n), out_shape=(pltpu.VMEM((rows,...]
    unnamed x2 -> x0, local copies, waits for them, and re-layouts: 1.44 us -> none
    pallas_call x0 -> x1, Pallas kernels: none -> 0.84 us  [kernel_body(): pl.pallas_call(write_out, out_shape=(jax.ShapeDtypeStruct(acc.shape, f32)...]
where the time goes in v9:
time: 27.4 us; the launch traced here: 27.2 us
  Pallas kernels  26.6 us (97%)
  between operations  0.64 us (2%)
    pallas_call x1, Pallas kernels, kernel_body(): pl.pallas_call(functools.partial(kernel, n), out_shape=(pltpu.VMEM((rows,...  25.8 us
    pallas_call x1, Pallas kernels, kernel_body(): pl.pallas_call(write_out, out_shape=(jax.ShapeDtypeStruct(acc.shape, f32)...  0.84 us

profile of v9, /device:TPU:0, one launch (start us, length us, event | category | flops | bytes accessed | tf_op | source)
XLA Modules:
  0.0 27.2 jit_solution(7216169220254833121)
XLA Ops:
  0.6 25.8 %shard_map.77 = (f32[32,32,80]{2,1,0:T(8,128)S(1)}, f32[80,320]{1,0:T(8,128)S(1)}) custom-call(s32[64]{0:T(128)} %step_in.1, s32[64]{0:T(128)} %reach_in.1, f32[32,4,640]{2,1,0:T(4,128)} %saved_in.1, f32[32,4,640]{2,1,0:T(4,128)} %cot_in.1, f32[640,640]{1,0:T(8,128)} %weight_in.1, f32[27,64,80]{2,1,0:T(8,128)} %coefs_in.1), custom_call_target="tpu_custom_call" | custom-call | tf_op jit(solution)/shard_map/pallas_call | solution.py:313
  26.4 0.8 %shard_map.78 = (f32[32,32,80]{2,1,0:T(8,128)}, f32[80,320]{1,0:T(8,128)}) custom-call(f32[32,32,80]{2,1,0:T(8,128)S(1)} %get-tuple-element.6.acc_in, f32[80,320]{1,0:T(8,128)S(1)} %get-tuple-element.7.grad_in), custom_call_target="tpu_custom_call" | custom-call | tf_op jit(solution)/shard_map/pallas_call | solution.py:358

commit v10 on v9

--- a/solution.py
+++ b/solution.py
@@ -11,9 +11,9 @@
 MESH = pl.DeviceIdType.MESH
 REACH = 4
 MOST_STEP = 8
-WEIGHT_PARTS = 4
+SLAB = 256
 SUBLANES = 8
-WINDOW = 2
+WINDOW = 1
 LANES = 128
 
 
@@ -68,12 +68,12 @@
     bits = n.bit_length() - 1
     full, tail = divmod(half, LANES)
 
-    slab = channels // WEIGHT_PARTS
+    slabs = [(at, min(SLAB, channels - at)) for at in range(0, channels, SLAB)]
     pairs = [(saved_in, saved_ref)]
-    pairs += [(weight_in.at[pl.ds(i * slab, slab)], weight_ref.at[pl.ds(i * slab, slab)]) for i in range(WEIGHT_PARTS)]
+    pairs += [(weight_in.at[pl.ds(at, size)], weight_ref.at[pl.ds(at, size)]) for at, size in slabs]
     pairs += [(cot_in, cot_ref), (coefs_in, coefs_ref), (step_in, step_ref), (reach_in, reach_ref)]
     loads = [pltpu.make_async_copy(src, dst, load_sem.at[i]) for i, (src, dst) in enumerate(pairs)]
-    late = WEIGHT_PARTS + 2
+    late = len(slabs) + 2
     for load in loads[:late]:
         load.start()
 
@@ -85,14 +85,17 @@
     loads[0].wait()
     saved = saved_ref[...].reshape(cells, channels)
     s_t[...] = saved.T.reshape(n, own, cells)
-    for load in loads[1 : 1 + WEIGHT_PARTS]:
+    pieces = []
+    hidden = None
+    for (at, size), load in zip(slabs, loads[1:]):
         load.wait()
+        pieces.append(halves(weight_ref[at : at + size]))
+        term = dot3(halves(saved[:, at : at + size]), pieces[-1], ((1,), (0,)))
+        hidden = term if hidden is None else hidden + term
+    weight_high[...] = jnp.concatenate([p[0] for p in pieces], axis=0).reshape(n, own, channels)
+    weight_low[...] = jnp.concatenate([p[1] for p in pieces], axis=0).reshape(n, own, channels)
     for load in loads[late:]:
         load.start()
-    weight = halves(weight_ref[...])
-    weight_high[...] = weight[0].reshape(n, own, channels)
-    weight_low[...] = weight[1].reshape(n, own, channels)
-    hidden = dot3(halves(saved), weight, ((1,), (0,)))
     pl.semaphore_wait(barrier, n)
 
     def to_peer(src, dst, slot):
@@ -104,7 +107,7 @@
     saved_copy = to_peer(s_t, s_t_peer, 0)
     saved_copy.start()
 
-    loads[1 + WEIGHT_PARTS].wait()
+    loads[late - 1].wait()
     pre_grad = cot_ref[...].reshape(cells, channels) * gelu_slope(hidden)
     turned = pre_grad.T
     pg_t[...] = turned.reshape(2, half, cells)
@@ -325,7 +328,7 @@
             pltpu.VMEM(cotangent.shape, f32),
             pltpu.VMEM(weight.shape, f32),
             pltpu.VMEM(coefs.shape, f32),
-            pltpu.SemaphoreType.DMA((WEIGHT_PARTS + 5,)),
+            pltpu.SemaphoreType.DMA((5 + -(-weight.shape[0] // SLAB),)),
             pltpu.VMEM((n, own, cells), f32),
             pltpu.VMEM((n, own, cells), f32),
             pltpu.VMEM((2, half, cells), f32),
@@ -468,7 +471,6 @@
         and rows >= 2 * REACH
         and 2 * cols == SUBLANES
         and n * cols >= 2 * MOST_STEP
-        and channels % (SUBLANES * WEIGHT_PARTS) == 0
     )
     run = kernel_body if fits else collective_body
     return run(saved, cotangent, weight, coefs, lon_step, row_reach)

time: 27.4 us -> 26.2 us (0.956)
  Pallas kernels: 26.6 us -> 25.4 us
    pallas_call x1, Pallas kernels: 25.8 us -> 24.6 us  [kernel_body(): pl.pallas_call(functools.partial(kernel, n), out_shape=(pltpu.VMEM((rows,...]
where the time goes in v10:
time: 26.2 us; the launch traced here: 26.1 us
  Pallas kernels  25.4 us (97%)
  between operations  0.64 us (2%)
    pallas_call x1, Pallas kernels, kernel_body(): pl.pallas_call(functools.partial(kernel, n), out_shape=(pltpu.VMEM((rows,...  24.6 us
    pallas_call x1, Pallas kernels, kernel_body(): pl.pallas_call(write_out, out_shape=(jax.ShapeDtypeStruct(acc.shape, f32)...  0.84 us

profile of v10, /device:TPU:0, one launch (start us, length us, event | category | flops | bytes accessed | tf_op | source)
XLA Modules:
  0.0 26.1 jit_solution(2344484553865900386)
XLA Ops:
  0.6 24.6 %shard_map.77 = (f32[32,32,80]{2,1,0:T(8,128)S(1)}, f32[80,320]{1,0:T(8,128)S(1)}) custom-call(s32[64]{0:T(128)} %step_in.1, s32[64]{0:T(128)} %reach_in.1, f32[32,4,640]{2,1,0:T(4,128)} %saved_in.1, f32[32,4,640]{2,1,0:T(4,128)} %cot_in.1, f32[640,640]{1,0:T(8,128)} %weight_in.1, f32[27,64,80]{2,1,0:T(8,128)} %coefs_in.1), custom_call_target="tpu_custom_call" | custom-call | tf_op jit(solution)/shard_map/pallas_call | solution.py:316
  25.2 0.8 %shard_map.78 = (f32[32,32,80]{2,1,0:T(8,128)}, f32[80,320]{1,0:T(8,128)}) custom-call(f32[32,32,80]{2,1,0:T(8,128)S(1)} %get-tuple-element.6.acc_in, f32[80,320]{1,0:T(8,128)S(1)} %get-tuple-element.7.grad_in), custom_call_target="tpu_custom_call" | custom-call | tf_op jit(solution)/shard_map/pallas_call | solution.py:361

commit v11 on v10

--- a/solution.py
+++ b/solution.py
@@ -194,12 +194,16 @@
     def _(i):
         taps_of(REACH + i)
 
-    for at, even in enumerate(order[n // 2 : -1]):
+    def advance(at):
         if at + WINDOW < n // 2:
             sends[order[at]].wait_send()
             sends[order[at + WINDOW]].start()
+        even = order[n // 2 + at]
         part[even] = gather(even)
         sends[even].start()
+
+    for at in range(n // 2 - 2):
+        advance(at)
 
     slots[me] = cell[me].T
     for s in range(1, n):
@@ -225,6 +229,7 @@
         device_id={"lat": other}, device_id_type=MESH,
     )
     halo_copy.start()
+    advance(n // 2 - 2)
 
     def roll_row(values, place):
         step = jnp.full(values.shape, step_ref[lat * rows + place - REACH], jnp.int32)

time: 26.2 us -> 25.9 us (0.989)
  Pallas kernels: 25.4 us -> 25.1 us
    pallas_call x1, Pallas kernels: 24.6 us -> 24.2 us  [kernel_body(): pl.pallas_call(functools.partial(kernel, n), out_shape=(pltpu.VMEM((rows,...]
where the time goes in v11:
time: 25.9 us; the launch traced here: 25.7 us
  Pallas kernels  25.1 us (97%)
  between operations  0.64 us (2%)
    pallas_call x1, Pallas kernels, kernel_body(): pl.pallas_call(functools.partial(kernel, n), out_shape=(pltpu.VMEM((rows,...  24.2 us
    pallas_call x1, Pallas kernels, kernel_body(): pl.pallas_call(write_out, out_shape=(jax.ShapeDtypeStruct(acc.shape, f32)...  0.84 us

profile of v11, /device:TPU:0, one launch (start us, length us, event | category | flops | bytes accessed | tf_op | source)
XLA Modules:
  0.0 25.7 jit_solution(15253412107895267986)
XLA Ops:
  0.6 24.2 %shard_map.77 = (f32[32,32,80]{2,1,0:T(8,128)S(1)}, f32[80,320]{1,0:T(8,128)S(1)}) custom-call(s32[64]{0:T(128)} %step_in.1, s32[64]{0:T(128)} %reach_in.1, f32[32,4,640]{2,1,0:T(4,128)} %saved_in.1, f32[32,4,640]{2,1,0:T(4,128)} %cot_in.1, f32[640,640]{1,0:T(8,128)} %weight_in.1, f32[27,64,80]{2,1,0:T(8,128)} %coefs_in.1), custom_call_target="tpu_custom_call" | custom-call | tf_op jit(solution)/shard_map/pallas_call | solution.py:321
  24.9 0.8 %shard_map.78 = (f32[32,32,80]{2,1,0:T(8,128)}, f32[80,320]{1,0:T(8,128)}) custom-call(f32[32,32,80]{2,1,0:T(8,128)S(1)} %get-tuple-element.6.acc_in, f32[80,320]{1,0:T(8,128)S(1)} %get-tuple-element.7.grad_in), custom_call_target="tpu_custom_call" | custom-call | tf_op jit(solution)/shard_map/pallas_call | solution.py:366
